TPU v7x, 32 devices: a whole 2x2x4 slice. The times are simulated.
32 devices in a mesh: section: 4 (over x, core), tensor: 4 (over z), dp: 2 (over y).
Axes of the slice: x: 2, y: 2, z: 4, core: 2. Of those that a mesh axis runs over, the one named last changes fastest.
Arguments:
- act_inbox: bfloat16 [4, 1024, 16384], P('section', 'dp', 'tensor'), may hold values from -6 to 6
- grad_inbox: bfloat16 [4, 1024, 16384], P('section', 'dp', 'tensor'), may hold values from -0.125 to 0.125
- queries: bfloat16 [4, 1024, 16384], P('section', 'dp', 'tensor'), may hold values from -400 to 400
- keys_values: bfloat16 [4, 2, 1024, 1024], P('section', None, 'dp', 'tensor'), may hold values from -6 to 6
- saved_attn: bfloat16 [4, 1024, 16384], P('section', 'dp', 'tensor'), may hold values from -6 to 6
- down_adapt: bfloat16 [4, 8, 16, 16384], P('section', None, None, 'tensor'), may hold values from -0.375 to 0.375
- up_adapt: bfloat16 [4, 8, 16, 16384], P('section', None, None, 'tensor'), may hold values from -0.75 to 0.75
- seg_blocks: int32 [4, 2, 2, 3], P('section', None, 'dp'), may hold values from 1 to 4, 8 in all within a row
- seg_pads: int32 [4, 2, 2, 3], P('section', None, 'dp'), may hold values from 0 to 63
- seg_tenant: int32 [4, 2, 2, 3], P('section', None, 'dp'), may hold values from 0 to 31
- adapter_table: int32 [32], replicated, may hold values from 0 to 7
Outputs:
- new_acts: bfloat16 [4, 1024, 16384], P('section', 'dp', 'tensor')
- grad_down: bfloat16 [4, 8, 16, 16384], P('section', None, None, 'tensor')
- grad_up: bfloat16 [4, 8, 16, 16384], P('section', None, None, 'tensor')
Inputs may be any that keep to these rules, and one draw needn't show every extreme that they name: `seg_blocks`: each row of 3 block counts sums to 8.
All inputs are finite; a program needn't handle non-finite values.
Results may differ from a plain program's by a relative error of at most 0.0058.
Values may be sent and summed in bfloat16 or wider, within the bound.
A program may use at most 128 MiB of HBM per device.

v0:
```python
import math

import jax
import jax.numpy as jnp
from jax import lax
from jax.sharding import PartitionSpec as P

HD = 128
BLOCK = 64


adapter_scale = 2.0


def from_behind(value, axis, steps):
    count = lax.axis_size(axis)
    pairs = [(source, (source + steps) % count) for source in range(count)]
    return lax.ppermute(value, axis, pairs)


def token_layout(blocks, padding, tenants, slot_table, length, slot_count):
    positions = jnp.arange(length, dtype=jnp.int32)
    seg_ends = jnp.cumsum(blocks) * BLOCK
    segment = jnp.sum((positions[:, None] >= seg_ends[None, :]).astype(jnp.int32), axis=1)
    member = (segment[:, None] == jnp.arange(blocks.shape[0], dtype=jnp.int32)[None, :]).astype(
        jnp.int32
    )
    live_end = jnp.sum(member * (seg_ends - padding)[None, :], axis=1)
    alive = positions < live_end
    tenant_pick = (
        tenants[:, None] == jnp.arange(slot_table.shape[0], dtype=jnp.int32)[None, :]
    ).astype(jnp.int32)
    seg_slot = jnp.sum(tenant_pick * slot_table[None, :], axis=1)
    token_slot = jnp.sum(member * seg_slot[None, :], axis=1)
    onehot = (token_slot[:, None] == jnp.arange(slot_count, dtype=jnp.int32)[None, :]).astype(
        jnp.float32
    )
    return (segment, alive, onehot)


def attend(queries, keys_values, segment, alive):
    length = queries.shape[0]
    kv_width = keys_values.shape[-1]
    kv_heads = kv_width // HD
    group_size = queries.shape[1] // kv_width
    query_heads = queries.reshape(length, kv_heads, group_size, HD)
    key_heads = keys_values[0].reshape(length, kv_heads, HD)
    value_heads = keys_values[1].reshape(length, kv_heads, HD)
    positions = jnp.arange(length, dtype=jnp.int32)
    inv_root = 1.0 / math.sqrt(HD)

    def one_block(block_index):
        block_start = block_index * length
        block_pos = block_start + jnp.arange(length, dtype=jnp.int32)
        scores = (
            jnp.einsum("qhgd,khd->hgqk", query_heads, key_heads, preferred_element_type=jnp.float32)
            * inv_root
        )
        allowed = (segment[:, None] == segment[None, :]) & (
            block_pos[:, None] >= positions[None, :]
        )
        allowed = allowed & alive[None, :] & alive[:, None]
        masked_scores = jnp.where(allowed, scores, -1e30)
        row_top = jnp.max(masked_scores, axis=-1, keepdims=True)
        exponent = jnp.where(allowed, jnp.exp(masked_scores - row_top), 0.0)
        row_total = jnp.sum(exponent, axis=-1, keepdims=True)
        row_total = jnp.where(alive[None, None, :, None], row_total, 1.0)
        weights = (exponent / row_total).astype(jnp.bfloat16)
        attended = jnp.einsum(
            "hgqk,khd->qhgd", weights, value_heads, preferred_element_type=jnp.float32
        )
        return attended.astype(jnp.bfloat16).reshape(length, kv_heads * group_size * HD)

    blocks_out = lax.map(one_block, jnp.arange(length // length, dtype=jnp.int32))
    return blocks_out.reshape(length, -1)


def project_rows(left, right):
    return lax.dot_general(
        left, right, (((1,), (1,)), ((), ())), preferred_element_type=jnp.float32
    )


def contract(left, right):
    return lax.dot_general(
        left, right, (((0,), (0,)), ((), ())), preferred_element_type=jnp.float32
    )


def select_slots(full, onehot):
    return jnp.sum(full.reshape(full.shape[0], onehot.shape[1], -1) * onehot[:, :, None], axis=1)


def spread_tokens(ranked, onehot):
    wide = onehot[:, :, None] * ranked.astype(jnp.float32)[:, None, :]
    return wide.reshape(ranked.shape[0], -1).astype(jnp.bfloat16)


def per_device(
    act_inbox,
    grad_inbox,
    queries,
    keys_values,
    saved_attn,
    down_adapt,
    up_adapt,
    seg_blocks,
    seg_pads,
    seg_tenant,
    adapter_table,
):
    received_input = from_behind(act_inbox[0], "section", 1)
    returned = from_behind(grad_inbox[0], "section", -1)
    length = received_input.shape[0]
    slot_count = up_adapt.shape[1]
    down_rows = down_adapt[0].reshape(-1, down_adapt.shape[-1])
    upward_rows = up_adapt[0].reshape(-1, up_adapt.shape[-1])
    segment, alive, onehot = token_layout(
        seg_blocks[0, 0, 0],
        seg_pads[0, 0, 0],
        seg_tenant[0, 0, 0],
        adapter_table,
        length,
        slot_count,
    )
    back_seg, back_alive, backward_slot_mask = token_layout(
        seg_blocks[0, 1, 0],
        seg_pads[0, 1, 0],
        seg_tenant[0, 1, 0],
        adapter_table,
        length,
        slot_count,
    )
    saved_rows = saved_attn[0]
    masked_scores = returned * back_alive[:, None].astype(jnp.bfloat16)
    back_part = select_slots(project_rows(saved_rows, down_rows), backward_slot_mask)
    grad_part = select_slots(project_rows(masked_scores, upward_rows), backward_slot_mask)
    attended = attend(queries[0], keys_values[0], segment, alive)
    fwd_part = select_slots(project_rows(attended, down_rows), onehot)
    back_sum, gradient_total = lax.psum((back_part, grad_part), "tensor")
    fwd_sum = lax.psum(fwd_part, "tensor")
    adapter_update = jnp.dot(
        spread_tokens(fwd_sum.astype(jnp.bfloat16), onehot),
        upward_rows,
        preferred_element_type=jnp.float32,
    )
    summed_output = received_input.astype(jnp.float32) + adapter_scale * adapter_update
    new_acts = summed_output.astype(jnp.bfloat16)
    spread_rank = spread_tokens(back_sum.astype(jnp.bfloat16), backward_slot_mask)
    spread_gradient = spread_tokens(
        (adapter_scale * gradient_total).astype(jnp.bfloat16), backward_slot_mask
    )
    grad_d, up_gradient = lax.psum(
        (contract(spread_gradient, saved_rows), contract(spread_rank, masked_scores)), "dp"
    )
    output_layout = up_adapt.shape
    return (
        new_acts[None],
        grad_d.reshape(output_layout).astype(jnp.bfloat16),
        (adapter_scale * up_gradient).reshape(output_layout).astype(jnp.bfloat16),
    )


def solution(mesh):
    placed = (
        P("section", "dp", "tensor"),
        P("section", "dp", "tensor"),
        P("section", "dp", "tensor"),
        P("section", None, "dp", "tensor"),
        P("section", "dp", "tensor"),
        P("section", None, None, "tensor"),
        P("section", None, None, "tensor"),
        P("section", None, "dp", None),
        P("section", None, "dp", None),
        P("section", None, "dp", None),
        P(),
    )
    return jax.shard_map(
        per_device,
        mesh=mesh,
        in_specs=placed,
        out_specs=(
            P("section", "dp", "tensor"),
            P("section", None, None, "tensor"),
            P("section", None, None, "tensor"),
        ),
        check_vma=False,
    )
```

profile of v0, /device:TPU:0, one launch (start us, length us, event | category | flops | bytes accessed | tf_op | source)
XLA Modules:
  0.0 237.2 jit_solution(8647438626208774221)
XLA Ops:
  7.2 0.0 copy-start
  7.2 0.0 all-reduce.5.cloned.1.call-start
  7.2 2.4 %collective-permute-start.1 = (bf16[512,4096]{1,0:T(8,128)(2,1)}, bf16[512,4096]{1,0:T(8,128)(2,1)}, u32[]{:S(2)}, u32[]{:S(2)}) collective-permute-start(bf16[512,4096]{1,0:T(8,128)(2,1)} %bitcast.103), channel_id=1, source_target_pairs={{0,24},{8,0},{16,8},{24,16},{1,25},{9,1},{17,9},{25,17},{2,26},{10... | collective-permute-start | bytes 12582920 | tf_op jit(solution)/shard_map/ppermute | solution.py:18
  9.7 0.0 collective-permute-start
  9.7 1.1 fusion.53
  10.7 0.1 copy.27
  10.9 0.7 slice_bitcast_fusion.1
  11.6 0.2 reduce-window.14
  11.7 0.1 convert_reduce_fusion.1
  11.8 0.7 slice_bitcast_fusion.2
  12.5 0.2 reduce-window.15
  12.7 0.1 convert_reduce_fusion
  12.8 0.7 bitcast_subtract_fusion
  13.4 0.9 select_reduce_fusion.4
  14.3 0.1 select_reduce_fusion.1
  14.4 0.2 fusion.46
  14.7 0.1 copy.37
  14.8 5.5 %copy.38 = bf16[64,8,32,128]{3,2,1,0:T(8,128)(2,1)} copy(bf16[64,8,32,128]{3,1,2,0:T(8,128)(2,1)} %bitcast.94) | data formatting | bytes 8388608
  20.3 22.3 %fusion.54 = (f32[2,16,512]{2,1,0:T(8,128)S(1)}, f32[2,16,512,512]{2,3,1,0:T(8,128)}) fusion(pred[512,512]{0,1:T(8,128)(4,1)S(1)} %fusion.46, bf16[512,2,128,1]{0,2,3,1:T(8,128)(2,1)S(1)} %bitcast.102, bf16[512,2,16,128]{3,2,1,0:T(8,128)(2,1)} %bitcast.95), kind=kOutput, calls=%fused_computation.81 | convolution fusion | flops 2189427200 | bytes 38338560 | tf_op jit(solution)/shard_map/while/body/eval_jaxpr/sub | solution.py:65
  42.6 0.0 copy-start.2
  42.6 14.0 %fusion.25 = bf16[2,16,512,128]{2,3,1,0:T(8,128)(2,1)} fusion(bf16[512,2,128,1]{0,2,3,1:T(8,128)(2,1)S(1)} %bitcast.101, f32[2,16,512,512]{2,3,1,0:T(8,128)} %get-tuple-element.47, f32[2,16,512]{2,1,0:T(8,128)S(1)} %broadcast_select_fusion), kind=kOutput, calls=%fused_computation.24 | convolution fusion | flops 2166358016 | bytes 38076416 | tf_op jit(solution)/shard_map/while/body/eval_jaxpr/hgqk,khd->qhgd/dot_general | solution.py:69
  56.6 0.0 copy-done.2
  56.6 0.0 copy-start.1
  56.6 3.1 %fusion.37 = f32[512,16]{0,1:T(8,128)S(1)} fusion(bf16[512,4096,1]{0,1,2:T(8,128)(2,1)} %bitcast.105, bf16[1,8,16,4096]{3,2,1,0:T(8,128)(2,1)S(1)} %copy-done.2, f32[512,8]{0,1:T(8,128)S(1)} %fusion.48), kind=kOutput, calls=%fused_computation.32 | convolution fusion | flops 536993792 | bytes 5292032 | tf_op jit(solution)/shard_map/dot_general | solution.py:79
  59.7 0.4 copy-done.1
  60.1 1.6 fusion.34
  61.7 39.2 %collective-permute-done.1 = bf16[512,4096]{1,0:T(8,128)(2,1)} collective-permute-done((bf16[512,4096]{1,0:T(8,128)(2,1)}, bf16[512,4096]{1,0:T(8,128)(2,1)}, u32[]{:S(2)}, u32[]{:S(2)}) %collective-permute-start.1) | collective-permute-done | bytes 4194336 | tf_op jit(solution)/shard_map/ppermute | solution.py:18
  100.9 0.0 copy-done
  100.9 3.8 %fusion.38 = f32[512,16]{0,1:T(8,128)S(1)} fusion(bf16[512,4096]{1,0:T(8,128)(2,1)} %collective-permute-done.1, bf16[512]{0:T(512)(128)(2,1)S(1)} %fusion.50, bf16[1,8,16,4096]{3,2,1,0:T(8,128)(2,1)S(1)} %copy-done, f32[512,8]{0,1:T(8,128)S(1)} %fusion.49), kind=kOutput, calls=%fused_computation.33 | convolution fusion | flops 545382400 | bytes 5293056 | tf_op jit(solution)/shard_map/dot_general | solution.py:79
  104.7 20.5 %all-reduce.6 = (bf16[512,16]{0,1:T(8,128)(2,1)S(1)}, f32[512,16]{0,1:T(8,128)S(1)}, bf16[512,16]{0,1:T(8,128)(2,1)S(1)}) all-reduce(f32[512,16]{0,1:T(8,128)S(1)} %fusion.37, f32[512,16]{0,1:T(8,128)S(1)} %fusion.38, f32[512,16]{0,1:T(8,128)S(1)} %fusion.34), channel_id=1, replica_groups=mesh['section'=4,'tensor'=4,'dp'=2] {'tensor'}, use_global_device_ids=true, to_apply=%region_8.9 | all-reduce | flops 24576 | bytes 163840 | tf_op jit(solution)/shard_map/psum | solution.py:141
  125.3 3.0 %fusion.11 = f32[128,4096]{1,0:T(8,128)S(1)} fusion(bf16[512,128]{0,1:T(8,128)(2,1)S(1)} %bitcast.100, bf16[1,512,4096]{2,1,0:T(8,128)(2,1)} %param.15), kind=kOutput, calls=%fused_computation.14 | convolution fusion | flops 536870912 | bytes 6422528 | tf_op jit(solution)/shard_map/dot_general | solution.py:85
  128.2 4.3 %fusion.22 = f32[128,4096]{1,0:T(8,128)} fusion(bf16[512,128]{0,1:T(8,128)(2,1)S(1)} %bitcast.99, bf16[512,4096]{1,0:T(8,128)(2,1)} %collective-permute-done.1, bf16[512]{0:T(512)(128)(2,1)S(1)} %fusion.50), kind=kOutput, calls=%fused_computation.21 | convolution fusion | flops 538968064 | bytes 6423552 | tf_op jit(solution)/shard_map/dot_general | solution.py:85
  132.6 0.0 all-reduce.5.cloned.1.call-update
  132.6 0.0 collective-permute-done
  132.7 5.5 %fusion.8 = bf16[1,512,4096]{2,1,0:T(8,128)(2,1)} fusion(bf16[512,128]{0,1:T(8,128)(2,1)S(1)} %bitcast.98, bf16[128,4096]{1,0:T(8,128)(2,1)S(1)} %bitcast.93, bf16[512,4096]{1,0:T(8,128)(2,1)} %collective-permute-done), kind=kOutput, calls=%fused_computation.11 | convolution fusion | flops 545259520 | bytes 9568256 | tf_op jit(solution)/shard_map/dot_general | solution.py:142
  138.1 83.8 %all-reduce.7 = bf16[128,4096]{1,0:T(8,128)(2,1)} all-reduce(f32[128,4096]{1,0:T(8,128)S(1)} %fusion.11), channel_id=1, replica_groups=mesh['section'=4,'tensor'=4,'dp'=2] {'dp'}, use_global_device_ids=true, to_apply=%region_16.17 | all-reduce | flops 524288 | bytes 3145728 | tf_op jit(solution)/shard_map/psum | solution.py:153
  221.9 5.7 %all-reduce.5.cloned.1.call-done = f32[128,4096]{1,0:T(8,128)} async-done(((f32[128,4096]{1,0:T(8,128)}), f32[128,4096]{1,0:T(8,128)}) %all-reduce.5.cloned.1.call-update) | async-done | bytes 2097168 | tf_op jit(solution)/shard_map/psum | solution.py:153
  227.7 2.7 %multiply_convert_fusion = bf16[128,4096]{1,0:T(8,128)(2,1)} fusion(f32[128,4096]{1,0:T(8,128)} %all-reduce.5.cloned.1.call-done), kind=kLoop, calls=%fused_computation.25 | loop fusion | flops 1048576 | bytes 3145728 | tf_op jit(solution)/shard_map/convert_element_type | solution.py:160
  (12 shorter events, 0.1 us)
Async XLA Ops:
  7.2 93.7 %copy-start = (bf16[1,8,16,4096]{3,2,1,0:T(8,128)(2,1)S(1)}, bf16[1,8,16,4096]{3,2,1,0:T(8,128)(2,1)}, u32[]{:S(2)}) copy-start(bf16[1,8,16,4096]{3,2,1,0:T(8,128)(2,1)} %param.17) | copy-start | bytes 3145732
  7.2 220.5 %all-reduce.5.cloned.1.call-start = ((), (), s32[]{:S(2)}) async-start(), calls=%async_computation | async-start | bytes 4194304 | tf_op jit(solution)/shard_map/psum | solution.py:153
  7.2 93.7 %collective-permute-start.1 = (bf16[512,4096]{1,0:T(8,128)(2,1)}, bf16[512,4096]{1,0:T(8,128)(2,1)}, u32[]{:S(2)}, u32[]{:S(2)}) collective-permute-start(bf16[512,4096]{1,0:T(8,128)(2,1)} %bitcast.103), channel_id=1, source_target_pairs={{0,24},{8,0},{16,8},{24,16},{1,25},{9,1},{17,9},{25,17},{2,26},{10... | collective-permute-start | bytes 12582920 | tf_op jit(solution)/shard_map/ppermute | solution.py:18
  9.7 123.0 %collective-permute-start = (bf16[512,4096]{1,0:T(8,128)(2,1)}, bf16[512,4096]{1,0:T(8,128)(2,1)}, u32[]{:S(2)}, u32[]{:S(2)}) collective-permute-start(bf16[512,4096]{1,0:T(8,128)(2,1)} %bitcast.104), channel_id=1, source_target_pairs={{0,8},{8,16},{16,24},{24,0},{1,9},{9,17},{17,25},{25,1},{2,10},{10... | collective-permute-start | bytes 12582920 | tf_op jit(solution)/shard_map/ppermute | solution.py:18
  42.6 14.0 %copy-start.2 = (bf16[1,8,16,4096]{3,2,1,0:T(8,128)(2,1)S(1)}, bf16[1,8,16,4096]{3,2,1,0:T(8,128)(2,1)}, u32[]{:S(2)}) copy-start(bf16[1,8,16,4096]{3,2,1,0:T(8,128)(2,1)} %param.16) | copy-start | bytes 3145732
  56.6 3.5 %copy-start.1 = (bf16[1,512,4096]{2,1,0:T(8,128)(2,1)S(1)}, bf16[1,512,4096]{2,1,0:T(8,128)(2,1)}, u32[]{:S(2)}) copy-start(bf16[1,512,4096]{2,1,0:T(8,128)(2,1)} %param.15) | copy-start | bytes 12582916
Sparse Core Ops, SparseCore 0:
  132.7 94.8 all-reduce.4
where the time goes:
time: 238 us; the launch traced here: 237 us
  blocking collectives  104 us (44%)
  matrix products  57.5 us (24%)
  waiting for transfers between devices  44.9 us (19%)
  between operations  14.2 us (6%)
  local copies, waits for them, and re-layouts  8.55 us (4%)
  other arithmetic  5.24 us (2%)
  starting transfers between devices  2.47 us (1%)
    psum x1, blocking collectives, per_device(): lax.psum((contract(spread_gradient, saved_rows), contract(spread_rank, ma...  83.8 us
    ppermute x2, waiting for transfers between devices, from_behind(): return lax.ppermute(value, axis, pairs)  39.2 us
    sub x1, matrix products, one_block(): exponent = jnp.where(allowed, jnp.exp(masked_scores - row_top), 0.0)  22.3 us
    psum x1, blocking collectives, per_device(): fwd_sum = lax.psum(fwd_part, 'tensor')  20.5 us
    dot_general x1, matrix products, one_block(): jnp.einsum('hgqk,khd->qhgd', weights, value_heads, preferred_element_type...  14 us
    dot_general x3, matrix products, project_rows(): lax.dot_general(left, right, (((1,), (1,)), ((), ())), preferred_element_...  8.43 us
    dot_general x2, matrix products, contract(): lax.dot_general(left, right, (((0,), (0,)), ((), ())), preferred_element_...  7.29 us
    unnamed x8, local copies, waits for them, and re-layouts  6 us
  transfers between devices with their start and end apart: 3, of which 2 were waited for; matrix products, arithmetic and copies ran while one was open for 29% of the time, Pallas kernels for 0%

commit v1 on v0

v1 whole, which is shorter than its diff:
```python
import functools
import math

import jax
import jax.numpy as jnp
from jax import lax
from jax.experimental import pallas as pl
from jax.experimental.pallas import tpu as pltpu
from jax.sharding import PartitionSpec as P

HD = 128
BLOCK = 64
MAX_SEG = 4 * BLOCK
TILE = 128
SCALE = 2.0
F32 = jnp.float32
BF16 = jnp.bfloat16
VMEM_BYTES = 48 * 1024 * 1024

SMEM = pl.BlockSpec(memory_space=pltpu.SMEM)


def dot(left, right, dims):
    return lax.dot_general(left, right, ((dims[:1], dims[1:]), ((), ())), preferred_element_type=F32)


def seg_bounds(blocks, pads, batch):
    bounds, start = [], 0
    for i in range(blocks.shape[-1]):
        end = start + blocks[0, batch, 0, i] * BLOCK
        bounds.append((start, end, end - pads[0, batch, 0, i]))
        start = end
    return bounds


def seg_slots(tenant, table, batch):
    return [table[tenant[0, batch, 0, i]] for i in range(tenant.shape[-1])]


def by_segment(pos, bounds, values):
    out = jnp.zeros_like(pos) + values[0]
    for (start, _, _), value in zip(bounds[1:], values[1:]):
        out = jnp.where(pos >= start, value, out)
    return out


def select_rows(full, keys, key_row, rank):
    out = jnp.zeros((rank, full.shape[1]), F32)
    for i, key in enumerate(keys):
        out = out + jnp.where(key_row == key, full[i * rank : (i + 1) * rank], 0.0)
    return out


def spread_rows(ranked, keys, key_row):
    return jnp.concatenate([jnp.where(key_row == key, ranked, 0.0) for key in keys], axis=0)


def token_row(length):
    return lax.broadcasted_iota(jnp.int32, (1, length), 1)


def pack_up_kernel(tenant, table, up, out):
    rank = up.shape[2]
    for i, slot in enumerate(seg_slots(tenant, table, 1)):
        out[i * rank : (i + 1) * rank, :] = up[0, slot]


def saved_rank_kernel(blocks, pads, tenant, table, saved, down, out, acc):
    step = pl.program_id(0)
    slots, rank = down.shape[1], down.shape[2]

    @pl.when(step == 0)
    def _():
        acc[...] = jnp.zeros_like(acc)

    acc[...] += dot(saved[0], down[0].reshape(slots * rank, -1), (1, 1))

    @pl.when(step == pl.num_programs(0) - 1)
    def _():
        bounds = seg_bounds(blocks, pads, 1)
        slot_row = by_segment(token_row(acc.shape[0]), bounds, seg_slots(tenant, table, 1))
        out[...] = select_rows(acc[...].T, range(slots), slot_row, rank)


def attend_kernel(blocks, pads, tenant, table, q, kv, down, out, acc, bias, live, v_ones, att):
    step = pl.program_id(0)
    length = q.shape[1]
    heads = q.shape[2] // HD
    slots, rank = down.shape[1], down.shape[2]
    factor = math.log2(math.e) / math.sqrt(HD)

    def window(tile):
        first = max(0, tile * TILE - MAX_SEG)
        return first, (tile + 1) * TILE

    @pl.when(step == 0)
    def _():
        acc[...] = jnp.zeros_like(acc)
        bounds = seg_bounds(blocks, pads, 0)
        v_ones[:, :HD] = kv[0, 1]
        v_ones[:, HD:] = jnp.ones((length, HD), BF16)
        for tile in range(length // TILE):
            first, last = window(tile)
            rows = tile * TILE + lax.broadcasted_iota(jnp.int32, (TILE, last - first), 0)
            cols = first + lax.broadcasted_iota(jnp.int32, (TILE, last - first), 1)
            starts = by_segment(rows, bounds, [b[0] for b in bounds])
            ends = by_segment(rows, bounds, [b[2] for b in bounds])
            seen = (cols >= starts) & (cols <= rows) & (cols < ends)
            bias[tile * TILE : (tile + 1) * TILE, : last - first] = jnp.where(seen, 0.0, -1e30)
            rows = tile * TILE + lax.broadcasted_iota(jnp.int32, (TILE, HD), 0)
            ends = by_segment(rows, bounds, [b[2] for b in bounds])
            live[tile * TILE : (tile + 1) * TILE, :] = jnp.where(rows < ends, 1.0, 0.0)

    for tile in range(length // TILE):
        first, last = window(tile)
        here = slice(tile * TILE, (tile + 1) * TILE)
        for pair in range(0, heads, 2):
            rows = jnp.concatenate(
                [q[0, here, h * HD : (h + 1) * HD] for h in (pair, pair + 1)], axis=0
            )
            scores = dot(rows, kv[0, 0, first:last, :], (1, 1)).reshape(2, TILE, last - first)
            scores = scores * factor + bias[here, : last - first][None]
            top = jnp.max(scores, axis=-1, keepdims=True)
            weights = jnp.exp2(scores - top).astype(BF16).reshape(2 * TILE, last - first)
            mixed = dot(weights, v_ones[first:last, :], (1, 0))
            for n, h in enumerate((pair, pair + 1)):
                part = mixed[n * TILE : (n + 1) * TILE]
                value = part[:, :HD] * (live[here, :] / part[:, HD:])
                att[here, h * HD : (h + 1) * HD] = value.astype(BF16)
    acc[...] += dot(att[...], down[0].reshape(slots * rank, -1), (1, 1))

    @pl.when(step == pl.num_programs(0) - 1)
    def _():
        bounds = seg_bounds(blocks, pads, 0)
        slot_row = by_segment(token_row(length), bounds, seg_slots(tenant, table, 0))
        out[...] = select_rows(acc[...].T, range(slots), slot_row, rank)


def grad_side_kernel(parts, blocks, pads, *refs):
    ranks, (grad, up, part_out, up_out, acc, spread) = refs[:parts], refs[parts:]
    step = pl.program_id(0)
    length = grad.shape[1]
    rank = part_out.shape[0]
    segs = up.shape[0] // rank
    bounds = seg_bounds(blocks, pads, 1)
    tokens = token_row(length)
    live = tokens < by_segment(tokens, bounds, [b[2] for b in bounds])
    seg_row = jnp.where(live, by_segment(tokens, bounds, list(range(segs))), -1)

    @pl.when(step == 0)
    def _():
        acc[...] = jnp.zeros_like(acc)
        total = sum(r[...] for r in ranks).astype(BF16).astype(F32)
        spread[...] = spread_rows(total, range(segs), seg_row).astype(BF16)

    block = grad[0]
    fill = jnp.zeros((acc.shape[1] - up.shape[0], up.shape[1]), BF16)
    acc[...] += dot(block, jnp.concatenate([up[...], fill], axis=0), (1, 1))
    up_out[...] = (SCALE * dot(spread[...], block, (1, 0))).astype(BF16)

    @pl.when(step == pl.num_programs(0) - 1)
    def _():
        part_out[...] = select_rows(acc[...].T, range(segs), seg_row, rank)


def grad_down_kernel(parts, blocks, pads, *refs):
    ranks, (saved, out, spread) = refs[:parts], refs[parts:]
    segs = blocks.shape[-1]

    @pl.when(pl.program_id(0) == 0)
    def _():
        bounds = seg_bounds(blocks, pads, 1)
        seg_row = by_segment(token_row(saved.shape[1]), bounds, list(range(segs)))
        total = (SCALE * sum(r[...] for r in ranks)).astype(BF16).astype(F32)
        spread[...] = spread_rows(total, range(segs), seg_row).astype(BF16)

    out[...] = dot(spread[...], saved[0], (1, 0)).astype(BF16)


def new_acts_kernel(parts, blocks, pads, tenant, table, *refs):
    ranks, (arrived, up, out, spread) = refs[:parts], refs[parts:]
    slots, rank = up.shape[1], up.shape[2]

    @pl.when(pl.program_id(0) == 0)
    def _():
        bounds = seg_bounds(blocks, pads, 0)
        slot_row = by_segment(token_row(arrived.shape[0]), bounds, seg_slots(tenant, table, 0))
        total = sum(r[...] for r in ranks).astype(BF16).astype(F32)
        spread[...] = spread_rows(total, range(slots), slot_row).T.astype(BF16)

    update = dot(spread[...], up[0].reshape(slots * rank, -1), (1, 0))
    out[0] = (arrived[...].astype(F32) + SCALE * update).astype(BF16)


def place_kernel(dp_axis, tenant, other_tenant, table, own_d, other_d, own_u, other_u, out_d, out_u):
    slots, rank = out_d.shape[1], out_d.shape[2]
    first = lax.axis_index(dp_axis) == 0
    own, other = seg_slots(tenant, table, 1), seg_slots(other_tenant, table, 1)
    keys = [jnp.where(first, a, b) for a, b in zip(own, other)]
    keys += [jnp.where(first, b, a) for a, b in zip(own, other)]
    for mine, peer, out in ((own_d, other_d, out_d), (own_u, other_u, out_u)):
        a, b = mine[...], peer[...]
        rows = jnp.concatenate([jnp.where(first, a, b), jnp.where(first, b, a)], axis=0)
        rows = rows.astype(F32)
        for slot in range(slots):
            total = jnp.zeros((rank, rows.shape[1]), F32)
            for i, key in enumerate(keys):
                total = total + jnp.where(key == slot, rows[i * rank : (i + 1) * rank], 0.0)
            out[0, slot] = total.astype(BF16)


def params(**more):
    return pltpu.CompilerParams(vmem_limit_bytes=VMEM_BYTES, **more)


def cost(flops, nbytes):
    return pl.CostEstimate(flops=flops, bytes_accessed=nbytes, transcendentals=0)


def whole(array):
    zeros = (0,) * array.ndim
    return pl.BlockSpec(array.shape, lambda *_: zeros)


def per_device(
    sizes,
    act_inbox,
    grad_inbox,
    queries,
    keys_values,
    saved_attn,
    down_adapt,
    up_adapt,
    seg_blocks,
    seg_pads,
    seg_tenant,
    adapter_table,
):
    n_section, n_tensor, n_dp = sizes["section"], sizes["tensor"], sizes["dp"]
    _, length, width = queries.shape
    _, slots, rank, _ = up_adapt.shape
    segs = seg_blocks.shape[-1]
    rows = slots * rank
    packed = segs * rank
    kv_heads = keys_values.shape[-1] // HD
    group = width // keys_values.shape[-1]
    meta = (seg_blocks, seg_pads, seg_tenant, adapter_table)
    half = pl.BlockSpec(memory_space=pltpu.VMEM)

    def section_shift(value, steps):
        pairs = [(i, (i + steps) % n_section) for i in range(n_section)]
        return lax.ppermute(value, "section", pairs)

    def dp_swap(value):
        return lax.ppermute(value, "dp", [(i, (i + 1) % n_dp) for i in range(n_dp)])

    def to_all_tensor(value, steps):
        got = []
        for k in range(n_tensor):
            if steps == 0 and k == 0:
                got.append(value)
                continue
            pairs = [
                (s * n_tensor + z, ((s + steps) % n_section) * n_tensor + (z + k) % n_tensor)
                for s in range(n_section)
                for z in range(n_tensor)
            ]
            got.append(lax.ppermute(value, ("section", "tensor"), pairs))
        return got

    arrived = section_shift(act_inbox[0], 1)

    up_packed = pl.pallas_call(
        pack_up_kernel,
        out_shape=jax.ShapeDtypeStruct((packed, width), BF16),
        in_specs=[SMEM, SMEM, half],
        out_specs=half,
        compiler_params=params(),
        cost_estimate=cost(0, 4 * packed * width),
        name="pack_up",
    )(seg_tenant, adapter_table, up_adapt)
    up_there = section_shift(up_packed, 1)
    blocks_there = section_shift(seg_blocks, 1)
    pads_there = section_shift(seg_pads, 1)

    cols = 1024
    steps = width // cols
    back_part = pl.pallas_call(
        saved_rank_kernel,
        grid=(steps,),
        out_shape=jax.ShapeDtypeStruct((rank, length), F32),
        in_specs=[SMEM] * 4
        + [
            pl.BlockSpec((1, length, cols), lambda i: (0, 0, i)),
            pl.BlockSpec((1, slots, rank, cols), lambda i: (0, 0, 0, i)),
        ],
        out_specs=pl.BlockSpec((rank, length), lambda i: (0, 0)),
        scratch_shapes=[pltpu.VMEM((length, rows), F32)],
        compiler_params=params(),
        cost_estimate=cost(2 * length * rows * width, 2 * length * width),
        name="saved_rank",
    )(*meta, saved_attn, down_adapt)
    back_parts = to_all_tensor(back_part, 1)

    heads = 4
    per_kv = group // heads

    def attend(kv_head):
        return pl.pallas_call(
            attend_kernel,
            grid=(per_kv,),
            out_shape=jax.ShapeDtypeStruct((rank, length), F32),
            in_specs=[SMEM] * 4
            + [
                pl.BlockSpec((1, length, heads * HD), lambda i: (0, 0, kv_head * per_kv + i)),
                pl.BlockSpec((1, 2, length, HD), lambda i: (0, 0, 0, kv_head)),
                pl.BlockSpec((1, slots, rank, heads * HD), lambda i: (0, 0, 0, kv_head * per_kv + i)),
            ],
            out_specs=pl.BlockSpec((rank, length), lambda i: (0, 0)),
            scratch_shapes=[
                pltpu.VMEM((length, rows), F32),
                pltpu.VMEM((length, MAX_SEG + TILE), F32),
                pltpu.VMEM((length, HD), F32),
                pltpu.VMEM((length, 2 * HD), BF16),
                pltpu.VMEM((length, heads * HD), BF16),
            ],
            compiler_params=params(),
            cost_estimate=cost(8 * length * length * group * HD, 2 * length * group * HD),
            name="attend",
        )(*meta, queries, keys_values, down_adapt)

    fwd_halves = [attend(0)]

    gated, back_parts, up_there = lax.optimization_barrier((grad_inbox, back_parts, up_there))
    grad_part, up_grad = pl.pallas_call(
        functools.partial(grad_side_kernel, n_tensor),
        grid=(steps,),
        out_shape=[
            jax.ShapeDtypeStruct((rank, length), F32),
            jax.ShapeDtypeStruct((packed, width), BF16),
        ],
        in_specs=[SMEM] * 2
        + [pl.BlockSpec((rank, length), lambda i: (0, 0))] * n_tensor
        + [
            pl.BlockSpec((1, length, cols), lambda i: (0, 0, i)),
            pl.BlockSpec((packed, cols), lambda i: (0, i)),
        ],
        out_specs=[
            pl.BlockSpec((rank, length), lambda i: (0, 0)),
            pl.BlockSpec((packed, cols), lambda i: (0, i)),
        ],
        scratch_shapes=[pltpu.VMEM((length, rows), F32), pltpu.VMEM((packed, length), BF16)],
        compiler_params=params(),
        cost_estimate=cost(4 * length * rows * width, 2 * length * width),
        name="grad_side",
    )(blocks_there, pads_there, *back_parts, gated, up_there)
    grad_parts = to_all_tensor(grad_part, -1)
    up_grad = section_shift(up_grad, -1)

    for kv_head in range(1, kv_heads):
        fwd_halves.append(attend(kv_head))
    fwd_parts = to_all_tensor(sum(fwd_halves), 0)

    down_grad = pl.pallas_call(
        functools.partial(grad_down_kernel, n_tensor),
        grid=(steps,),
        out_shape=jax.ShapeDtypeStruct((packed, width), BF16),
        in_specs=[SMEM] * 2
        + [pl.BlockSpec((rank, length), lambda i: (0, 0))] * n_tensor
        + [pl.BlockSpec((1, length, cols), lambda i: (0, 0, i))],
        out_specs=pl.BlockSpec((packed, cols), lambda i: (0, i)),
        scratch_shapes=[pltpu.VMEM((packed, length), BF16)],
        compiler_params=params(),
        cost_estimate=cost(2 * length * rows * width, 2 * length * width),
        name="grad_down",
    )(seg_blocks, seg_pads, *grad_parts, saved_attn)

    new_acts = pl.pallas_call(
        functools.partial(new_acts_kernel, n_tensor),
        grid=(steps,),
        out_shape=jax.ShapeDtypeStruct((1, length, width), BF16),
        in_specs=[SMEM] * 4
        + [pl.BlockSpec((rank, length), lambda i: (0, 0))] * n_tensor
        + [
            pl.BlockSpec((length, cols), lambda i: (0, i)),
            pl.BlockSpec((1, slots, rank, cols), lambda i: (0, 0, 0, i)),
        ],
        out_specs=pl.BlockSpec((1, length, cols), lambda i: (0, 0, i)),
        scratch_shapes=[pltpu.VMEM((length, rows), BF16)],
        compiler_params=params(),
        cost_estimate=cost(2 * length * rows * width, 4 * length * width),
        name="new_acts",
    )(*meta, *fwd_parts, arrived, up_adapt)

    if n_dp == 2:
        other_tenant = dp_swap(seg_tenant)
        other_up, other_down = dp_swap(up_grad), dp_swap(down_grad)
        block = pl.BlockSpec((packed, cols), lambda i: (0, i))
        out_block = pl.BlockSpec((1, slots, rank, cols), lambda i: (0, 0, 0, i))
        grad_down, grad_up = pl.pallas_call(
            functools.partial(place_kernel, "dp"),
            grid=(steps,),
            out_shape=[jax.ShapeDtypeStruct(up_adapt.shape, BF16)] * 2,
            in_specs=[SMEM] * 3 + [block] * 4,
            out_specs=[out_block] * 2,
            compiler_params=params(),
            cost_estimate=cost(0, 12 * rows * width),
            name="place",
        )(seg_tenant, other_tenant, adapter_table, down_grad, other_down, up_grad, other_up)
    else:
        seg_slot = adapter_table[seg_tenant[0, 1, 0]]
        onehot = (seg_slot[None, :] == jnp.arange(slots, dtype=jnp.int32)[:, None]).astype(F32)

        def placed(compact):
            full = jnp.einsum("as,srw->arw", onehot, compact.reshape(segs, rank, width).astype(F32))
            return lax.psum(full, "dp").astype(BF16)[None]

        grad_down, grad_up = placed(down_grad), placed(up_grad)
    return new_acts, grad_down, grad_up


def solution(mesh):
    wide = P("section", "dp", "tensor")
    adapter = P("section", None, None, "tensor")
    per_segment = P("section", None, "dp", None)
    return jax.shard_map(
        functools.partial(per_device, dict(mesh.shape)),
        mesh=mesh,
        in_specs=(
            wide,
            wide,
            wide,
            P("section", None, "dp", "tensor"),
            wide,
            adapter,
            adapter,
            per_segment,
            per_segment,
            per_segment,
            P(),
        ),
        out_specs=(wide, adapter, adapter),
        check_vma=False,
    )
```

time: 238 us -> 112 us (0.47)
  blocking collectives: 104 us -> 0 us
  matrix products: 57.5 us -> 0 us
  Pallas kernels: 0 us -> 32.1 us
  starting transfers between devices: 2.47 us -> 26.1 us
  between operations: 14.2 us -> 0.84 us
  other arithmetic: 5.24 us -> 0.01 us
  waiting for transfers between devices: 44.9 us -> 41.6 us
    psum x2 -> x0, blocking collectives: 104 us -> none  [the longest x1 83.8 us: per_device(): lax.psum((contract(spread_gradient, saved_rows), contract(spread_rank, ma...]
    dot_general x7 -> x0, matrix products: 35.2 us -> none  [the longest x1 14 us: one_block(): jnp.einsum('hgqk,khd->qhgd', weights, value_heads, preferred_element_type...]
    pallas_call x0 -> x8, Pallas kernels: none -> 32.1 us  [the longest x2 15.6 us: attend(): pl.pallas_call(attend_kernel, grid=(per_kv,), out_shape=jax.ShapeDtypeStr...]
    ppermute x2 -> x19, starting transfers between devices: 2.43 us -> 26.1 us  [the longest x11 15.3 us: to_all_tensor(): got.append(lax.ppermute(value, ('section', 'tensor'), pairs))]
    sub x1 -> x0, matrix products: 22.3 us -> none  [one_block(): exponent = jnp.where(allowed, jnp.exp(masked_scores - row_top), 0.0)]
    psum x1 -> x0, waiting for transfers between devices: 5.71 us -> none  [per_device(): lax.psum((contract(spread_gradient, saved_rows), contract(spread_rank, ma...]
    unnamed x8 -> x40, local copies, waits for them, and re-layouts: 6 us -> 10.9 us
    convert_element_type x9 -> x0, other arithmetic: 2.78 us -> none  [the longest x1 2.7 us: per_device(): (adapter_scale * up_gradient).reshape(output_layout).astype(jnp.bfloat16)]
  transfers between devices with their start and end apart: 3 -> 19, of which waited for: 2 -> 5; matrix products, arithmetic and copies ran while one was open for 29% -> 0% of each run, Pallas kernels for 0% -> 25%
where the time goes in v1:
time: 112 us
  waiting for transfers between devices  41.6 us (37%)
  Pallas kernels  32.1 us (29%)
  starting transfers between devices  26.1 us (23%)
  local copies, waits for them, and re-layouts  10.9 us (10%)
    ppermute x11, waiting for transfers between devices, to_all_tensor(): got.append(lax.ppermute(value, ('section', 'tensor'), pairs))  34.8 us
    pallas_call x2, Pallas kernels, attend(): pl.pallas_call(attend_kernel, grid=(per_kv,), out_shape=jax.ShapeDtypeStr...  15.6 us
    ppermute x11, starting transfers between devices, to_all_tensor(): got.append(lax.ppermute(value, ('section', 'tensor'), pairs))  15.3 us
    unnamed x40, local copies, waits for them, and re-layouts  10.9 us
    ppermute x5, starting transfers between devices, section_shift(): return lax.ppermute(value, 'section', pairs)  7.09 us
    pallas_call x1, Pallas kernels, per_device(): pl.pallas_call(functools.partial(new_acts_kernel, n_tensor), grid=(steps,...  4.18 us
    ppermute x3, waiting for transfers between devices, dp_swap(): return lax.ppermute(value, 'dp', [(i, (i + 1) % n_dp) for i in range(n_dp)])  3.83 us
    ppermute x3, starting transfers between devices, dp_swap(): return lax.ppermute(value, 'dp', [(i, (i + 1) % n_dp) for i in range(n_dp)])  3.68 us
  transfers between devices with their start and end apart: 19, of which 5 were waited for; matrix products, arithmetic and copies ran while one was open for 0% of the time, Pallas kernels for 25%

profile of v1, /device:TPU:0, one launch (start us, length us, event | category | flops | bytes accessed | tf_op | source)
XLA Modules:
  0.0 111.5 jit_solution(2301699869323389696)
XLA Ops:
  0.6 0.5 collective-permute-start.3
  1.1 1.2 %copy-done.3 = bf16[1,8,16,4096]{3,2,1,0:T(8,128)(2,1)S(1)} copy-done((bf16[1,8,16,4096]{3,2,1,0:T(8,128)(2,1)S(1)}, bf16[1,8,16,4096]{3,2,1,0:T(8,128)(2,1)}, u32[]{:S(2)}) %copy-start.3) | copy-done | bytes 1048600
  2.4 0.7 copy-done.7
  3.0 0.7 copy-done.14
  3.7 0.6 pack_up.1
  4.3 2.7 %collective-permute-start.11 = (bf16[48,4096]{1,0:T(8,128)(2,1)S(1)}, bf16[48,4096]{1,0:T(8,128)(2,1)S(1)}, u32[]{:S(2)}, u32[]{:S(2)}) collective-permute-start(bf16[48,4096]{1,0:T(8,128)(2,1)S(1)} %pack_up.1), channel_id=1, source_target_pairs={{0,8},{8,16},{16,24},{24,0},{1,9},{9,17},{17,25},{25,1},{2,10},{10... | collective-permute-start | bytes 1179656 | tf_op jit(solution)/shard_map/ppermute | solution.py:252
  6.9 2.2 %copy-done = bf16[1,512,4096]{2,1,0:T(8,128)(2,1)S(1)} copy-done((bf16[1,512,4096]{2,1,0:T(8,128)(2,1)S(1)}, bf16[1,512,4096]{2,1,0:T(8,128)(2,1)}, u32[]{:S(2)}) %copy-start) | copy-done | bytes 4194328
  9.1 1.2 %copy-done.5 = bf16[1,8,16,4096]{3,2,1,0:T(8,128)(2,1)S(1)} copy-done((bf16[1,8,16,4096]{3,2,1,0:T(8,128)(2,1)S(1)}, bf16[1,8,16,4096]{3,2,1,0:T(8,128)(2,1)}, u32[]{:S(2)}) %copy-start.5) | copy-done | bytes 1048600
  10.4 0.7 copy-done.8
  11.0 0.7 copy-done.10
  11.7 0.7 copy-done.12
  12.4 0.7 copy-done.15
  13.1 0.0 copy-start.19
  13.1 2.9 %saved_rank.1 = f32[16,512]{1,0:T(8,128)S(1)} custom-call(s32[1,2,1,3]{3,2,1,0:T(1,128)S(1)} %copy-done.10, s32[1,2,1,3]{3,2,1,0:T(1,128)S(1)} %copy-done.12, s32[1,2,1,3]{3,2,1,0:T(1,128)S(1)} %copy-done.8, s32[32]{0:T(128)S(1)} %copy-done.15, bf16[1,512,4096]{2,1,0:T(8,128)(2,1)S(1)} %copy-done, bf16[1,8,16,4096]{3,2,1,0:T(8,128)(2,1)S(1)} %copy-done.5), custom_call_target="tpu_custom_call" | custom-call | flops 536870912 | bytes 4194304 | tf_op jit(solution)/shard_map/saved_rank/pallas_call | solution.py:288
  16.0 0.1 collective-permute-start.7
  16.0 1.8 %collective-permute-start.8 = (f32[16,512]{1,0:T(8,128)S(1)}, f32[16,512]{1,0:T(8,128)S(1)}, u32[]{:S(2)}, u32[]{:S(2)}) collective-permute-start(f32[16,512]{1,0:T(8,128)S(1)} %saved_rank.1), channel_id=1, source_target_pairs={{0,10},{2,12},{4,14},{6,8},{8,18},{10,20},{12,22},{14,16},{16,26},... | collective-permute-start | bytes 98312 | tf_op jit(solution)/shard_map/ppermute | solution.py:268
  17.8 2.1 %collective-permute-start.9 = (f32[16,512]{1,0:T(8,128)S(1)}, f32[16,512]{1,0:T(8,128)S(1)}, u32[]{:S(2)}, u32[]{:S(2)}) collective-permute-start(f32[16,512]{1,0:T(8,128)S(1)} %saved_rank.1), channel_id=1, source_target_pairs={{0,12},{2,14},{4,8},{6,10},{8,20},{10,22},{12,16},{14,18},{16,28},... | collective-permute-start | bytes 98312 | tf_op jit(solution)/shard_map/ppermute | solution.py:268
  19.9 34.8 %collective-permute-done.7.refs_0_ = f32[16,512]{1,0:T(8,128)S(1)} collective-permute-done((f32[16,512]{1,0:T(8,128)S(1)}, f32[16,512]{1,0:T(8,128)S(1)}, u32[]{:S(2)}, u32[]{:S(2)}) %collective-permute-start.7) | collective-permute-done | bytes 32800 | tf_op jit(solution)/shard_map/ppermute | solution.py:268
  54.7 3.1 %collective-permute-start.10 = (f32[16,512]{1,0:T(8,128)S(1)}, f32[16,512]{1,0:T(8,128)S(1)}, u32[]{:S(2)}, u32[]{:S(2)}) collective-permute-start(f32[16,512]{1,0:T(8,128)S(1)} %saved_rank.1), channel_id=1, source_target_pairs={{0,14},{2,8},{4,10},{6,12},{8,22},{10,16},{12,18},{14,20},{16,30},... | collective-permute-start | bytes 98312 | tf_op jit(solution)/shard_map/ppermute | solution.py:268
  57.9 0.0 collective-permute-done.8.refs_1_
  57.9 2.3 %collective-permute-start.5 = (s32[1,2,1,3]{3,2,1,0:T(1,128)S(1)}, s32[1,2,1,3]{3,2,1,0:T(1,128)S(1)}, u32[]{:S(2)}, u32[]{:S(2)}) collective-permute-start(s32[1,2,1,3]{3,2,1,0:T(1,128)S(1)} %copy-done.10), channel_id=1, source_target_pairs={{0,8},{8,16},{16,24},{24,0},{1,9},{9,17},{17,25},{25,1},{2,10},{10... | collective-permute-start | bytes 80 | tf_op jit(solution)/shard_map/ppermute | solution.py:252
  60.2 0.0 collective-permute-done.9.refs_2_
  60.2 0.1 collective-permute-start.6
  60.2 0.0 collective-permute-done.10.refs_3_
  60.2 0.0 collective-permute-done.11.refs_5_
  60.3 1.3 %collective-permute-done.5.blocks = s32[1,2,1,3]{3,2,1,0:T(1,128)S(1)} collective-permute-done((s32[1,2,1,3]{3,2,1,0:T(1,128)S(1)}, s32[1,2,1,3]{3,2,1,0:T(1,128)S(1)}, u32[]{:S(2)}, u32[]{:S(2)}) %collective-permute-start.5) | collective-permute-done | bytes 56 | tf_op jit(solution)/shard_map/ppermute | solution.py:252
  61.6 1.6 %collective-permute-done.6.pads = s32[1,2,1,3]{3,2,1,0:T(1,128)S(1)} collective-permute-done((s32[1,2,1,3]{3,2,1,0:T(1,128)S(1)}, s32[1,2,1,3]{3,2,1,0:T(1,128)S(1)}, u32[]{:S(2)}, u32[]{:S(2)}) %collective-permute-start.6) | collective-permute-done | bytes 56 | tf_op jit(solution)/shard_map/ppermute | solution.py:252
  63.2 3.3 %grad_side.1 = (f32[16,512]{1,0:T(8,128)S(1)}, bf16[48,4096]{1,0:T(8,128)(2,1)S(1)}) custom-call(s32[1,2,1,3]{3,2,1,0:T(1,128)S(1)} %collective-permute-done.5.blocks, s32[1,2,1,3]{3,2,1,0:T(1,128)S(1)} %collective-permute-done.6.pads, f32[16,512]{1,0:T(8,128)S(1)} %collective-permute-done.7.refs_0_, f32[16,512]{1,0:T(8,128)S(1)} %collective-permute-done.8.refs_1_, ...), custom_call_target="tpu_custom_call" | custom-call | flops 1073741824 | bytes 4194304 | tf_op jit(solution)/shard_map/grad_side/pallas_call | solution.py:335
  66.5 0.1 collective-permute-start.12
  66.6 0.1 collective-permute-start.13
  66.6 3.2 %collective-permute-start.14 = (f32[16,512]{1,0:T(8,128)S(1)}, f32[16,512]{1,0:T(8,128)S(1)}, u32[]{:S(2)}, u32[]{:S(2)}) collective-permute-start(f32[16,512]{1,0:T(8,128)S(1)} %get-tuple-element.19), channel_id=1, source_target_pairs={{0,28},{2,30},{4,24},{6,26},{8,4},{10,6},{12,0},{14,2},{16,12},{18... | collective-permute-start | bytes 98312 | tf_op jit(solution)/shard_map/ppermute | solution.py:268
  69.9 0.2 collective-permute-start.15
  70.1 0.0 collective-permute-done.12.refs_0_
  70.1 1.6 %collective-permute-start.17 = (bf16[48,4096]{1,0:T(8,128)(2,1)S(1)}, bf16[48,4096]{1,0:T(8,128)(2,1)S(1)}, u32[]{:S(2)}, u32[]{:S(2)}) collective-permute-start(bf16[48,4096]{1,0:T(8,128)(2,1)S(1)} %get-tuple-element.20), channel_id=1, source_target_pairs={{0,24},{8,0},{16,8},{24,16},{1,25},{9,1},{17,9},{25,17},{2,26},{10... | collective-permute-start | bytes 1179656 | tf_op jit(solution)/shard_map/ppermute | solution.py:252
  71.7 0.0 copy-done.6
  71.7 0.0 copy-done.11
  71.7 0.0 copy-start.17
  71.7 2.2 %copy-done.17 = bf16[1,512,4096]{2,1,0:T(8,128)(2,1)S(1)} copy-done((bf16[1,512,4096]{2,1,0:T(8,128)(2,1)S(1)}, bf16[1,512,4096]{2,1,0:T(8,128)(2,1)}, u32[]{:S(2)}) %copy-start.17) | copy-done | bytes 4194328
  73.9 7.8 %attend.2 = f32[16,512]{1,0:T(8,128)S(1)} custom-call(s32[1,2,1,3]{3,2,1,0:T(1,128)S(1)} %copy-done.11, s32[1,2,1,3]{3,2,1,0:T(1,128)S(1)} %copy-done.13, s32[1,2,1,3]{3,2,1,0:T(1,128)S(1)} %copy-done.9, s32[32]{0:T(128)S(1)} %copy-done.16, bf16[1,512,4096]{2,1,0:T(8,128)(2,1)S(1)} %copy-done.17, bf16[1,2,512,256]{3,2,1,0:T(8,128)(2,1)S(1)} %copy-done.19, ...), custom_call_target="tpu_custom_call" | custom-call | flops 4294967296 | bytes 2097152 | tf_op jit(solution)/shard_map/attend/pallas_call | solution.py:309
  81.7 0.0 copy-start.18
  81.7 0.0 collective-permute-done.13.refs_1_
  81.7 1.6 %collective-permute-start.4 = (s32[1,2,1,3]{3,2,1,0:T(1,128)S(1)}, s32[1,2,1,3]{3,2,1,0:T(1,128)S(1)}, u32[]{:S(2)}, u32[]{:S(2)}) collective-permute-start(s32[1,2,1,3]{3,2,1,0:T(1,128)S(1)} %copy-done.9), channel_id=1, source_target_pairs={{0,1},{1,0},{2,3},{3,2},{4,5},{5,4},{6,7},{7,6},{8,9},{9,8},{10,11... | collective-permute-start | bytes 80 | tf_op jit(solution)/shard_map/ppermute | solution.py:255
  83.3 0.0 collective-permute-done.14.refs_2_
  83.3 0.0 collective-permute-done.15.refs_3_
  83.3 0.0 copy-done.1
  83.3 2.1 %grad_down.1.own_d = bf16[48,4096]{1,0:T(8,128)(2,1)S(1)} custom-call(s32[1,2,1,3]{3,2,1,0:T(1,128)S(1)} %copy-done.11, s32[1,2,1,3]{3,2,1,0:T(1,128)S(1)} %copy-done.13, f32[16,512]{1,0:T(8,128)S(1)} %collective-permute-done.12.refs_0_, f32[16,512]{1,0:T(8,128)S(1)} %collective-permute-done.13.refs_1_, f32[16,512]{1,0:T(8,128)S(1)} %collective-permute-done.14.refs_2_, ...), custom_call_target="tpu_custom_call" | custom-call | flops 536870912 | bytes 4194304 | tf_op jit(solution)/shard_map/grad_down/pallas_call | solution.py:364
  85.4 0.0 copy-start.4
  85.4 0.6 collective-permute-start.16
  86.0 0.0 collective-permute-done.17.own_u
  86.0 1.5 %collective-permute-start.18 = (bf16[48,4096]{1,0:T(8,128)(2,1)S(1)}, bf16[48,4096]{1,0:T(8,128)(2,1)S(1)}, u32[]{:S(2)}, u32[]{:S(2)}) collective-permute-start(bf16[48,4096]{1,0:T(8,128)(2,1)S(1)} %collective-permute-done.17.own_u), channel_id=1, source_target_pairs={{0,1},{1,0},{2,3},{3,2},{4,5},{5,4},{6,7},{7,6},{8,9},{9,8},{10,11... | collective-permute-start | bytes 1179656 | tf_op jit(solution)/shard_map/ppermute | solution.py:255
  87.5 0.0 copy-done.18
  87.5 7.8 %attend.3 = f32[16,512]{1,0:T(8,128)S(1)} custom-call(s32[1,2,1,3]{3,2,1,0:T(1,128)S(1)} %copy-done.11, s32[1,2,1,3]{3,2,1,0:T(1,128)S(1)} %copy-done.13, s32[1,2,1,3]{3,2,1,0:T(1,128)S(1)} %copy-done.9, s32[32]{0:T(128)S(1)} %copy-done.16, bf16[1,512,4096]{2,1,0:T(8,128)(2,1)S(1)} %copy-done.18, bf16[1,2,512,256]{3,2,1,0:T(8,128)(2,1)S(1)} %copy-done.19, ...), custom_call_target="tpu_custom_call" | custom-call | flops 4294967296 | bytes 2097152 | tf_op jit(solution)/shard_map/attend/pallas_call | solution.py:309
  95.3 0.9 collective-permute-start
  96.2 0.0 collective-permute-done.4.other_tenant
  96.2 1.1 collective-permute-start.1
  97.3 0.2 collective-permute-done.16.other_d
  97.5 2.6 %collective-permute-start.2 = (f32[16,512]{1,0:T(8,128)S(1)}, f32[16,512]{1,0:T(8,128)S(1)}, u32[]{:S(2)}, u32[]{:S(2)}) collective-permute-start(f32[16,512]{1,0:T(8,128)S(1)} %add.3.refs_0_), channel_id=1, source_target_pairs={{0,6},{2,0},{4,2},{6,4},{8,14},{10,8},{12,10},{14,12},{16,22},{18,... | collective-permute-start | bytes 98312 | tf_op jit(solution)/shard_map/ppermute | solution.py:268
  100.2 3.6 %collective-permute-done.18.other_u = bf16[48,4096]{1,0:T(8,128)(2,1)S(1)} collective-permute-done((bf16[48,4096]{1,0:T(8,128)(2,1)S(1)}, bf16[48,4096]{1,0:T(8,128)(2,1)S(1)}, u32[]{:S(2)}, u32[]{:S(2)}) %collective-permute-start.18) | collective-permute-done | bytes 393248 | tf_op jit(solution)/shard_map/ppermute | solution.py:255
  103.8 3.6 %place.1 = (bf16[1,8,16,4096]{3,2,1,0:T(8,128)(2,1)}, bf16[1,8,16,4096]{3,2,1,0:T(8,128)(2,1)}) custom-call(s32[1,2,1,3]{3,2,1,0:T(1,128)S(1)} %copy-done.9, s32[1,2,1,3]{3,2,1,0:T(1,128)S(1)} %collective-permute-done.4.other_tenant, s32[32]{0:T(128)S(1)} %copy-done.16, bf16[48,4096]{1,0:T(8,128)(2,1)S(1)} %grad_down.1.own_d, ...), custom_call_target="tpu_custom_call" | custom-call | bytes 6291456 | tf_op jit(solution)/shard_map/place/pallas_call | solution.py:400
  107.3 0.0 collective-permute-done.refs_1_
  107.3 0.0 collective-permute-done.1.refs_2_
  107.3 0.0 collective-permute-done.2.refs_3_
  107.3 0.0 collective-permute-done.3.refs_4_
  107.4 4.2 %new_acts.1 = bf16[1,512,4096]{2,1,0:T(8,128)(2,1)} custom-call(s32[1,2,1,3]{3,2,1,0:T(1,128)S(1)} %copy-done.11, s32[1,2,1,3]{3,2,1,0:T(1,128)S(1)} %copy-done.13, s32[1,2,1,3]{3,2,1,0:T(1,128)S(1)} %copy-done.9, s32[32]{0:T(128)S(1)} %copy-done.16, f32[16,512]{1,0:T(8,128)S(1)} %add.3.refs_0_, f32[16,512]{1,0:T(8,128)S(1)} %collective-permute-done.refs_1_, ...), custom_call_target="tpu_custom_call" | custom-call | flops 536870912 | bytes 8388608 | tf_op jit(solution)/shard_map/new_acts/pallas_call | solution.py:378
  (23 shorter events, 0.0 us)
Async XLA Ops:
  0.6 106.7 %collective-permute-start.3 = (bf16[512,4096]{1,0:T(8,128)(2,1)}, bf16[512,4096]{1,0:T(8,128)(2,1)S(1)}, u32[]{:S(2)}, u32[]{:S(2)}) collective-permute-start(bf16[512,4096]{1,0:T(8,128)(2,1)} %bitcast.1), channel_id=1, source_target_pairs={{0,8},{8,16},{16,24},{24,0},{1,9},{9,17},{17,25},{25,1},{2,10},{10... | collective-permute-start | bytes 12582920 | tf_op jit(solution)/shard_map/ppermute | solution.py:252
  1.1 1.2 %copy-start.3 = (bf16[1,8,16,4096]{3,2,1,0:T(8,128)(2,1)S(1)}, bf16[1,8,16,4096]{3,2,1,0:T(8,128)(2,1)}, u32[]{:S(2)}) copy-start(bf16[1,8,16,4096]{3,2,1,0:T(8,128)(2,1)} %up.1) | copy-start | bytes 3145732
  2.4 0.7 copy-start.7
  3.0 0.7 copy-start.14
  4.3 56.0 %collective-permute-start.11 = (bf16[48,4096]{1,0:T(8,128)(2,1)S(1)}, bf16[48,4096]{1,0:T(8,128)(2,1)S(1)}, u32[]{:S(2)}, u32[]{:S(2)}) collective-permute-start(bf16[48,4096]{1,0:T(8,128)(2,1)S(1)} %pack_up.1), channel_id=1, source_target_pairs={{0,8},{8,16},{16,24},{24,0},{1,9},{9,17},{17,25},{25,1},{2,10},{10... | collective-permute-start | bytes 1179656 | tf_op jit(solution)/shard_map/ppermute | solution.py:252
  6.9 2.2 %copy-start = (bf16[1,512,4096]{2,1,0:T(8,128)(2,1)S(1)}, bf16[1,512,4096]{2,1,0:T(8,128)(2,1)}, u32[]{:S(2)}) copy-start(bf16[1,512,4096]{2,1,0:T(8,128)(2,1)} %refs_4_.2) | copy-start | bytes 12582916
  9.1 1.2 %copy-start.5 = (bf16[1,8,16,4096]{3,2,1,0:T(8,128)(2,1)S(1)}, bf16[1,8,16,4096]{3,2,1,0:T(8,128)(2,1)}, u32[]{:S(2)}) copy-start(bf16[1,8,16,4096]{3,2,1,0:T(8,128)(2,1)} %down.5) | copy-start | bytes 3145732
  10.4 0.7 copy-start.8
  11.0 0.7 copy-start.10
  11.7 0.7 copy-start.12
  12.4 0.7 copy-start.15
  13.0 50.1 %copy-start.2 = (bf16[1,512,4096]{2,1,0:T(8,128)(2,1)S(1)}, bf16[1,512,4096]{2,1,0:T(8,128)(2,1)}, u32[]{:S(2)}) copy-start(bf16[1,512,4096]{2,1,0:T(8,128)(2,1)} %refs_4_.1) | copy-start | bytes 12582916
  13.0 58.6 %copy-start.6 = (bf16[1,8,16,4096]{3,2,1,0:T(8,128)(2,1)S(1)}, bf16[1,8,16,4096]{3,2,1,0:T(8,128)(2,1)}, u32[]{:S(2)}) copy-start(bf16[1,8,16,4096]{3,2,1,0:T(8,128)(2,1)} %down.5) | copy-start | bytes 3145732
  13.1 58.6 %copy-start.9 = (s32[1,2,1,3]{3,2,1,0:T(1,128)S(1)}, s32[1,2,1,3]{3,2,1,0:T(1,128)}, u32[]{:S(2)}) copy-start(s32[1,2,1,3]{3,2,1,0:T(1,128)} %tenant.11) | copy-start | bytes 76
  13.1 58.6 %copy-start.11 = (s32[1,2,1,3]{3,2,1,0:T(1,128)S(1)}, s32[1,2,1,3]{3,2,1,0:T(1,128)}, u32[]{:S(2)}) copy-start(s32[1,2,1,3]{3,2,1,0:T(1,128)} %blocks.9) | copy-start | bytes 76
  13.1 58.6 %copy-start.13 = (s32[1,2,1,3]{3,2,1,0:T(1,128)S(1)}, s32[1,2,1,3]{3,2,1,0:T(1,128)}, u32[]{:S(2)}) copy-start(s32[1,2,1,3]{3,2,1,0:T(1,128)} %pads.9) | copy-start | bytes 76
  13.1 58.6 %copy-start.16 = (s32[32]{0:T(128)S(1)}, s32[32]{0:T(128)}, u32[]{:S(2)}) copy-start(s32[32]{0:T(128)} %table.11) | copy-start | bytes 388
  13.1 58.6 %copy-start.19 = (bf16[1,2,512,256]{3,2,1,0:T(8,128)(2,1)S(1)}, bf16[1,2,512,256]{3,2,1,0:T(8,128)(2,1)}, u32[]{:S(2)}) copy-start(bf16[1,2,512,256]{3,2,1,0:T(8,128)(2,1)} %kv.3) | copy-start | bytes 1572868
  16.0 38.8 %collective-permute-start.7 = (f32[16,512]{1,0:T(8,128)S(1)}, f32[16,512]{1,0:T(8,128)S(1)}, u32[]{:S(2)}, u32[]{:S(2)}) collective-permute-start(f32[16,512]{1,0:T(8,128)S(1)} %saved_rank.1), channel_id=1, source_target_pairs={{0,8},{2,10},{4,12},{6,14},{8,16},{10,18},{12,20},{14,22},{16,24},... | collective-permute-start | bytes 98312 | tf_op jit(solution)/shard_map/ppermute | solution.py:268
  16.0 41.8 %collective-permute-start.8 = (f32[16,512]{1,0:T(8,128)S(1)}, f32[16,512]{1,0:T(8,128)S(1)}, u32[]{:S(2)}, u32[]{:S(2)}) collective-permute-start(f32[16,512]{1,0:T(8,128)S(1)} %saved_rank.1), channel_id=1, source_target_pairs={{0,10},{2,12},{4,14},{6,8},{8,18},{10,20},{12,22},{14,16},{16,26},... | collective-permute-start | bytes 98312 | tf_op jit(solution)/shard_map/ppermute | solution.py:268
  17.8 42.3 %collective-permute-start.9 = (f32[16,512]{1,0:T(8,128)S(1)}, f32[16,512]{1,0:T(8,128)S(1)}, u32[]{:S(2)}, u32[]{:S(2)}) collective-permute-start(f32[16,512]{1,0:T(8,128)S(1)} %saved_rank.1), channel_id=1, source_target_pairs={{0,12},{2,14},{4,8},{6,10},{8,20},{10,22},{12,16},{14,18},{16,28},... | collective-permute-start | bytes 98312 | tf_op jit(solution)/shard_map/ppermute | solution.py:268
  54.7 5.5 %collective-permute-start.10 = (f32[16,512]{1,0:T(8,128)S(1)}, f32[16,512]{1,0:T(8,128)S(1)}, u32[]{:S(2)}, u32[]{:S(2)}) collective-permute-start(f32[16,512]{1,0:T(8,128)S(1)} %saved_rank.1), channel_id=1, source_target_pairs={{0,14},{2,8},{4,10},{6,12},{8,22},{10,16},{12,18},{14,20},{16,30},... | collective-permute-start | bytes 98312 | tf_op jit(solution)/shard_map/ppermute | solution.py:268
  57.9 3.7 %collective-permute-start.5 = (s32[1,2,1,3]{3,2,1,0:T(1,128)S(1)}, s32[1,2,1,3]{3,2,1,0:T(1,128)S(1)}, u32[]{:S(2)}, u32[]{:S(2)}) collective-permute-start(s32[1,2,1,3]{3,2,1,0:T(1,128)S(1)} %copy-done.10), channel_id=1, source_target_pairs={{0,8},{8,16},{16,24},{24,0},{1,9},{9,17},{17,25},{25,1},{2,10},{10... | collective-permute-start | bytes 80 | tf_op jit(solution)/shard_map/ppermute | solution.py:252
  60.2 3.0 %collective-permute-start.6 = (s32[1,2,1,3]{3,2,1,0:T(1,128)S(1)}, s32[1,2,1,3]{3,2,1,0:T(1,128)S(1)}, u32[]{:S(2)}, u32[]{:S(2)}) collective-permute-start(s32[1,2,1,3]{3,2,1,0:T(1,128)S(1)} %copy-done.12), channel_id=1, source_target_pairs={{0,8},{8,16},{16,24},{24,0},{1,9},{9,17},{17,25},{25,1},{2,10},{10... | collective-permute-start | bytes 80 | tf_op jit(solution)/shard_map/ppermute | solution.py:252
  66.5 3.6 %collective-permute-start.12 = (f32[16,512]{1,0:T(8,128)S(1)}, f32[16,512]{1,0:T(8,128)S(1)}, u32[]{:S(2)}, u32[]{:S(2)}) collective-permute-start(f32[16,512]{1,0:T(8,128)S(1)} %get-tuple-element.19), channel_id=1, source_target_pairs={{0,24},{2,26},{4,28},{6,30},{8,0},{10,2},{12,4},{14,6},{16,8},{18,... | collective-permute-start | bytes 98312 | tf_op jit(solution)/shard_map/ppermute | solution.py:268
  66.6 15.1 %collective-permute-start.13 = (f32[16,512]{1,0:T(8,128)S(1)}, f32[16,512]{1,0:T(8,128)S(1)}, u32[]{:S(2)}, u32[]{:S(2)}) collective-permute-start(f32[16,512]{1,0:T(8,128)S(1)} %get-tuple-element.19), channel_id=1, source_target_pairs={{0,26},{2,28},{4,30},{6,24},{8,2},{10,4},{12,6},{14,0},{16,10},{18... | collective-permute-start | bytes 98312 | tf_op jit(solution)/shard_map/ppermute | solution.py:268
  66.6 16.7 %collective-permute-start.14 = (f32[16,512]{1,0:T(8,128)S(1)}, f32[16,512]{1,0:T(8,128)S(1)}, u32[]{:S(2)}, u32[]{:S(2)}) collective-permute-start(f32[16,512]{1,0:T(8,128)S(1)} %get-tuple-element.19), channel_id=1, source_target_pairs={{0,28},{2,30},{4,24},{6,26},{8,4},{10,6},{12,0},{14,2},{16,12},{18... | collective-permute-start | bytes 98312 | tf_op jit(solution)/shard_map/ppermute | solution.py:268
  69.9 13.4 %collective-permute-start.15 = (f32[16,512]{1,0:T(8,128)S(1)}, f32[16,512]{1,0:T(8,128)S(1)}, u32[]{:S(2)}, u32[]{:S(2)}) collective-permute-start(f32[16,512]{1,0:T(8,128)S(1)} %get-tuple-element.19), channel_id=1, source_target_pairs={{0,30},{2,24},{4,26},{6,28},{8,6},{10,0},{12,2},{14,4},{16,14},{18... | collective-permute-start | bytes 98312 | tf_op jit(solution)/shard_map/ppermute | solution.py:268
  70.1 13.2 %copy-start.1 = (bf16[1,512,4096]{2,1,0:T(8,128)(2,1)S(1)}, bf16[1,512,4096]{2,1,0:T(8,128)(2,1)}, u32[]{:S(2)}) copy-start(bf16[1,512,4096]{2,1,0:T(8,128)(2,1)} %refs_4_.2) | copy-start | bytes 12582916
  70.1 15.9 %collective-permute-start.17 = (bf16[48,4096]{1,0:T(8,128)(2,1)S(1)}, bf16[48,4096]{1,0:T(8,128)(2,1)S(1)}, u32[]{:S(2)}, u32[]{:S(2)}) collective-permute-start(bf16[48,4096]{1,0:T(8,128)(2,1)S(1)} %get-tuple-element.20), channel_id=1, source_target_pairs={{0,24},{8,0},{16,8},{24,16},{1,25},{9,1},{17,9},{25,17},{2,26},{10... | collective-permute-start | bytes 1179656 | tf_op jit(solution)/shard_map/ppermute | solution.py:252
  71.7 2.2 %copy-start.17 = (bf16[1,512,4096]{2,1,0:T(8,128)(2,1)S(1)}, bf16[1,512,4096]{2,1,0:T(8,128)(2,1)}, u32[]{:S(2)}) copy-start(bf16[1,512,4096]{2,1,0:T(8,128)(2,1)} %q.3) | copy-start | bytes 12582916
  81.7 5.8 %copy-start.18 = (bf16[1,512,4096]{2,1,0:T(8,128)(2,1)S(1)}, bf16[1,512,4096]{2,1,0:T(8,128)(2,1)}, u32[]{:S(2)}) copy-start(bf16[1,512,4096]{2,1,0:T(8,128)(2,1)} %q.3) | copy-start | bytes 12582916
  81.7 14.5 %collective-permute-start.4 = (s32[1,2,1,3]{3,2,1,0:T(1,128)S(1)}, s32[1,2,1,3]{3,2,1,0:T(1,128)S(1)}, u32[]{:S(2)}, u32[]{:S(2)}) collective-permute-start(s32[1,2,1,3]{3,2,1,0:T(1,128)S(1)} %copy-done.9), channel_id=1, source_target_pairs={{0,1},{1,0},{2,3},{3,2},{4,5},{5,4},{6,7},{7,6},{8,9},{9,8},{10,11... | collective-permute-start | bytes 80 | tf_op jit(solution)/shard_map/ppermute | solution.py:255
  85.4 21.9 %copy-start.4 = (bf16[1,8,16,4096]{3,2,1,0:T(8,128)(2,1)S(1)}, bf16[1,8,16,4096]{3,2,1,0:T(8,128)(2,1)}, u32[]{:S(2)}) copy-start(bf16[1,8,16,4096]{3,2,1,0:T(8,128)(2,1)} %up.1) | copy-start | bytes 3145732
  85.4 12.1 %collective-permute-start.16 = (bf16[48,4096]{1,0:T(8,128)(2,1)S(1)}, bf16[48,4096]{1,0:T(8,128)(2,1)S(1)}, u32[]{:S(2)}, u32[]{:S(2)}) collective-permute-start(bf16[48,4096]{1,0:T(8,128)(2,1)S(1)} %grad_down.1.own_d), channel_id=1, source_target_pairs={{0,1},{1,0},{2,3},{3,2},{4,5},{5,4},{6,7},{7,6},{8,9},{9,8},{10,11... | collective-permute-start | bytes 1179656 | tf_op jit(solution)/shard_map/ppermute | solution.py:255
  86.0 17.8 %collective-permute-start.18 = (bf16[48,4096]{1,0:T(8,128)(2,1)S(1)}, bf16[48,4096]{1,0:T(8,128)(2,1)S(1)}, u32[]{:S(2)}, u32[]{:S(2)}) collective-permute-start(bf16[48,4096]{1,0:T(8,128)(2,1)S(1)} %collective-permute-done.17.own_u), channel_id=1, source_target_pairs={{0,1},{1,0},{2,3},{3,2},{4,5},{5,4},{6,7},{7,6},{8,9},{9,8},{10,11... | collective-permute-start | bytes 1179656 | tf_op jit(solution)/shard_map/ppermute | solution.py:255
  95.3 12.0 %collective-permute-start = (f32[16,512]{1,0:T(8,128)S(1)}, f32[16,512]{1,0:T(8,128)S(1)}, u32[]{:S(2)}, u32[]{:S(2)}) collective-permute-start(f32[16,512]{1,0:T(8,128)S(1)} %add.3.refs_0_), channel_id=1, source_target_pairs={{0,2},{2,4},{4,6},{6,0},{8,10},{10,12},{12,14},{14,8},{16,18},{18,... | collective-permute-start | bytes 98312 | tf_op jit(solution)/shard_map/ppermute | solution.py:268
  96.2 11.1 %collective-permute-start.1 = (f32[16,512]{1,0:T(8,128)S(1)}, f32[16,512]{1,0:T(8,128)S(1)}, u32[]{:S(2)}, u32[]{:S(2)}) collective-permute-start(f32[16,512]{1,0:T(8,128)S(1)} %add.3.refs_0_), channel_id=1, source_target_pairs={{0,4},{2,6},{4,0},{6,2},{8,12},{10,14},{12,8},{14,10},{16,20},{18,... | collective-permute-start | bytes 98312 | tf_op jit(solution)/shard_map/ppermute | solution.py:268
  97.5 9.8 %collective-permute-start.2 = (f32[16,512]{1,0:T(8,128)S(1)}, f32[16,512]{1,0:T(8,128)S(1)}, u32[]{:S(2)}, u32[]{:S(2)}) collective-permute-start(f32[16,512]{1,0:T(8,128)S(1)} %add.3.refs_0_), channel_id=1, source_target_pairs={{0,6},{2,0},{4,2},{6,4},{8,14},{10,8},{12,10},{14,12},{16,22},{18,... | collective-permute-start | bytes 98312 | tf_op jit(solution)/shard_map/ppermute | solution.py:268

commit v2 on v0

v2 whole, which is shorter than its diff:
```python
import functools
import math

import jax
import jax.numpy as jnp
from jax import lax
from jax.experimental import pallas as pl
from jax.experimental.pallas import tpu as pltpu
from jax.sharding import PartitionSpec as P

HD = 128
BLOCK = 64
MAX_SEG = 4 * BLOCK
TILE = 128
SCALE = 2.0
F32 = jnp.float32
BF16 = jnp.bfloat16
VMEM_BYTES = 60 * 1024 * 1024
CHUNK = 32
COLS = 1024
STEP_HEADS = 4

SMEM = pl.BlockSpec(memory_space=pltpu.SMEM)


def dot(left, right, dims):
    return lax.dot_general(left, right, ((dims[:1], dims[1:]), ((), ())), preferred_element_type=F32)


def seg_bounds(blocks, pads, batch):
    bounds, start = [], 0
    for i in range(blocks.shape[-1]):
        end = start + blocks[0, batch, 0, i] * BLOCK
        bounds.append((start, end, end - pads[0, batch, 0, i]))
        start = end
    return bounds


def seg_slots(tenant, table, batch):
    return [table[tenant[0, batch, 0, i]] for i in range(tenant.shape[-1])]


def by_segment(pos, bounds, values):
    out = jnp.zeros_like(pos) + values[0]
    for (start, _, _), value in zip(bounds[1:], values[1:]):
        out = jnp.where(pos >= start, value, out)
    return out


def select_rows(full, keys, key_row, rank):
    out = jnp.zeros((rank, full.shape[1]), F32)
    for i, key in enumerate(keys):
        out = out + jnp.where(key_row == key, full[i * rank : (i + 1) * rank], 0.0)
    return out


def spread_rows(ranked, keys, key_row):
    return jnp.concatenate([jnp.where(key_row == key, ranked, 0.0) for key in keys], axis=0)


def token_row(length):
    return lax.broadcasted_iota(jnp.int32, (1, length), 1)


class Kernel:
    def __init__(self, sizes, shapes):
        self.sections, self.tensors, self.dps = sizes["section"], sizes["tensor"], sizes["dp"]
        (_, self.length, self.width), self.kv_width, (_, self.slots, self.rank, _), self.segs = shapes
        self.rows = self.slots * self.rank
        self.packed = self.segs * self.rank
        self.kv_heads = self.kv_width // HD
        self.steps = self.width // (STEP_HEADS * HD)
        self.steps_per_kv = self.steps // self.kv_heads
        self.chunks = self.length // CHUNK

    def scratch(self):
        n, w, r, p = self.length, self.width, self.rank, self.packed
        dma = pltpu.SemaphoreType.DMA
        wide = pltpu.VMEM((n, w), BF16)
        adapter = pltpu.VMEM((self.slots, r, w), BF16)
        ranks = pltpu.VMEM((self.tensors, r, n), F32)
        one = pltpu.VMEM((r, n), F32)
        return dict(
            up_v=adapter,
            down_v=adapter,
            saved_v=wide,
            grad_v=wide,
            q_v=wide,
            kv_v=pltpu.VMEM((2, n, self.kv_width), BF16),
            up_send=pltpu.VMEM((p, w), BF16),
            up_in=pltpu.VMEM((p, w), BF16),
            tok=pltpu.VMEM((8, n), jnp.int32),
            tok_in=pltpu.VMEM((8, n), jnp.int32),
            tok_dp=pltpu.VMEM((self.dps, 8, n), jnp.int32),
            back_send=one,
            back_in=ranks,
            gp_send=one,
            gp_in=ranks,
            fwd_send=one,
            fwd_in=ranks,
            ug_send=pltpu.VMEM((p, w), BF16),
            ug_dp=pltpu.VMEM((self.dps, p, w), BF16),
            dg_dp=pltpu.VMEM((self.dps, p, w), BF16),
            arrived=wide,
            update=pltpu.VMEM((n, w), F32),
            acts_v=wide,
            gd_v=adapter,
            gu_v=adapter,
            acc=pltpu.VMEM((n, self.rows), F32),
            bias=pltpu.VMEM((n, MAX_SEG + TILE), F32),
            live=pltpu.VMEM((n, HD), F32),
            v_ones=pltpu.VMEM((self.kv_heads, n, 2 * HD), BF16),
            att=pltpu.VMEM((n, STEP_HEADS * HD), BF16),
            load_sem=dma((6,)),
            store_sem=dma((2,)),
            acts_sem=dma((self.chunks,)),
            up_sem=dma((2,)),
            tok_sem=dma((2,)),
            tok_dp_sem=dma((2, self.dps)),
            back_sem=dma((2, self.tensors)),
            gp_sem=dma((2, self.tensors)),
            fwd_sem=dma((2, self.tensors)),
            ug_sem=dma((2,)),
            ug_dp_sem=dma((2, self.dps)),
            dg_dp_sem=dma((2, self.dps)),
            act_sem=dma((2, self.chunks)),
        )

    def __call__(self, blocks, pads, tenant, table, act, grad, q, kv, saved, down, up, acts, gd, gu, **v):
        self.__dict__.update(v)
        self.meta = (blocks, pads, tenant, table)
        n, w, rank = self.length, self.width, self.rank
        me = {a: lax.axis_index(a) for a in ("section", "tensor", "dp")}

        def device(section=0, tensor=0, dp=0):
            return {
                "section": lax.rem(me["section"] + section + self.sections, self.sections),
                "tensor": lax.rem(me["tensor"] + tensor, self.tensors),
                "dp": lax.rem(me["dp"] + dp, self.dps),
            }

        def send(source, target, sems, where):
            return pltpu.make_async_remote_copy(
                src_ref=source,
                dst_ref=target,
                send_sem=sems[0],
                recv_sem=sems[1],
                device_id=where,
                device_id_type=pl.DeviceIdType.MESH,
            )

        def pair(sem, k):
            return sem.at[0, k], sem.at[1, k]

        def act_chunk(c):
            rows = pl.ds(pl.multiple_of(c * CHUNK, CHUNK), CHUNK)
            return send(
                act.at[0, rows, :], self.arrived.at[rows, :], pair(self.act_sem, c), device(section=1)
            )

        loads = [
            pltpu.make_async_copy(source, target, self.load_sem.at[i])
            for i, (source, target) in enumerate(
                (
                    (up.at[0], self.up_v),
                    (saved.at[0], self.saved_v),
                    (down.at[0], self.down_v),
                    (kv.at[0], self.kv_v),
                    (q.at[0], self.q_v),
                    (grad.at[0], self.grad_v),
                )
            )
        ]
        for load in loads:
            load.start()

        barrier = pltpu.get_barrier_semaphore()
        partners = [device(section=s, tensor=k) for s in (1, -1) for k in range(self.tensors)]
        partners += [device(tensor=k) for k in range(1, self.tensors)]
        partners += [device(dp=k) for k in range(1, self.dps)]
        for partner in partners:
            pl.semaphore_signal(
                barrier, inc=1, device_id=partner, device_id_type=pl.DeviceIdType.MESH
            )

        tokens = token_row(n)
        bounds = seg_bounds(blocks, pads, 1)
        slots = seg_slots(tenant, table, 1)
        alive = tokens < by_segment(tokens, bounds, [b[2] for b in bounds])
        line = lax.broadcasted_iota(jnp.int32, (8, n), 0)
        tok = jnp.where(alive, by_segment(tokens, bounds, list(range(self.segs))), -1) + 0 * line
        for i, slot in enumerate(slots):
            tok = jnp.where(line == i + 1, slot, tok)
        self.tok[...] = tok
        back_slot = by_segment(tokens, bounds, slots)

        loads[0].wait()
        for i, slot in enumerate(slots):
            self.up_send[i * rank : (i + 1) * rank, :] = self.up_v[slot]
        pl.semaphore_wait(barrier, len(partners))

        sent = []

        def start(copy):
            copy.start()
            sent.append(copy)
            return copy

        up_copy = start(send(self.up_send, self.up_in, (self.up_sem.at[0], self.up_sem.at[1]), device(section=1)))
        tok_copy = start(send(self.tok, self.tok_in, (self.tok_sem.at[0], self.tok_sem.at[1]), device(section=1)))
        act_chunk(0).start()
        tok_dp_copies = [
            start(send(self.tok, self.tok_dp.at[k], pair(self.tok_dp_sem, k), device(dp=k)))
            for k in range(1, self.dps)
        ]

        loads[1].wait()
        loads[2].wait()
        self.acc[...] = jnp.zeros_like(self.acc)

        @pl.loop(0, w // COLS)
        def _(i):
            cols = pl.ds(pl.multiple_of(i * COLS, COLS), COLS)
            right = self.down_v[:, :, cols].reshape(self.rows, COLS)
            self.acc[...] += dot(self.saved_v[:, cols], right, (1, 1))

        self.back_send[...] = select_rows(self.acc[...].T, range(self.slots), back_slot, rank)
        back_copies = [
            start(send(self.back_send, self.back_in.at[k], pair(self.back_sem, k), device(section=1, tensor=k)))
            for k in range(self.tensors)
        ]
        act_chunk(1).start()

        loads[3].wait()
        loads[4].wait()
        self.prepare_attention()
        self.acc[...] = jnp.zeros_like(self.acc)
        early, late = self.steps * 3 // 8, self.steps * 7 // 8

        def attend_steps(first, last):
            @pl.loop(first, last)
            def _(step):
                self.attend(step)
                act_chunk(2 + step).start()

        attend_steps(0, early)

        loads[5].wait()
        up_copy.wait_recv()
        tok_copy.wait_recv()
        for copy in back_copies:
            copy.wait_recv()
        seg_row = self.tok_in[0:1, :]
        total = sum(self.back_in[k] for k in range(self.tensors)).astype(BF16).astype(F32)
        spread = spread_rows(total, range(self.segs), seg_row).astype(BF16)
        fill = jnp.zeros((self.rows - self.packed, COLS), BF16)
        full = jnp.zeros((n, self.rows), F32)
        for i in range(w // COLS):
            cols = slice(i * COLS, (i + 1) * COLS)
            block = self.grad_v[:, cols]
            full = full + dot(block, jnp.concatenate([self.up_in[:, cols], fill], axis=0), (1, 1))
            self.ug_send[:, cols] = (SCALE * dot(spread, block, (1, 0))).astype(BF16)
        self.gp_send[...] = select_rows(full.T, range(self.segs), seg_row, rank)
        gp_copies = [
            start(send(self.gp_send, self.gp_in.at[k], pair(self.gp_sem, k), device(section=-1, tensor=k)))
            for k in range(self.tensors)
        ]
        ug_copy = start(send(self.ug_send, self.ug_dp.at[0], (self.ug_sem.at[0], self.ug_sem.at[1]), device(section=-1)))

        attend_steps(early, late)

        ug_copy.wait_recv()
        ug_dp_copies = [
            start(send(self.ug_dp.at[0], self.ug_dp.at[k], pair(self.ug_dp_sem, k), device(dp=k)))
            for k in range(1, self.dps)
        ]
        for copy in gp_copies:
            copy.wait_recv()
        total = SCALE * sum(self.gp_in[k] for k in range(self.tensors))
        spread = spread_rows(total.astype(BF16).astype(F32), range(self.segs), self.tok[0:1, :]).astype(BF16)
        for i in range(w // COLS):
            cols = slice(i * COLS, (i + 1) * COLS)
            self.dg_dp[0, :, cols] = dot(spread, self.saved_v[:, cols], (1, 0)).astype(BF16)
        dg_dp_copies = [
            start(send(self.dg_dp.at[0], self.dg_dp.at[k], pair(self.dg_dp_sem, k), device(dp=k)))
            for k in range(1, self.dps)
        ]

        attend_steps(late, self.steps)

        bounds = seg_bounds(blocks, pads, 0)
        fwd_slot = by_segment(tokens, bounds, seg_slots(tenant, table, 0))
        fwd_part = select_rows(self.acc[...].T, range(self.slots), fwd_slot, rank)
        self.fwd_send[...] = fwd_part
        fwd_copies = [
            start(send(self.fwd_send, self.fwd_in.at[k], pair(self.fwd_sem, k), device(tensor=k)))
            for k in range(1, self.tensors)
        ]
        for copy in fwd_copies:
            copy.wait_recv()
        total = fwd_part + sum(self.fwd_in[k] for k in range(1, self.tensors))
        total = total.astype(BF16).astype(F32)
        spread = spread_rows(total, range(self.slots), fwd_slot).T.astype(BF16)
        for i in range(w // COLS):
            cols = slice(i * COLS, (i + 1) * COLS)
            right = self.up_v[:, :, cols].reshape(self.rows, COLS)
            self.update[:, cols] = SCALE * dot(spread, right, (1, 0))

        issued = 2 + self.steps

        def acts_out(c):
            rows = pl.ds(pl.multiple_of(c * CHUNK, CHUNK), CHUNK)
            return pltpu.make_async_copy(self.acts_v.at[rows, :], acts.at[0, rows, :], self.acts_sem.at[c])

        def add_chunks(first, last):
            @pl.loop(first, last)
            def _(c):
                @pl.when(c + issued < self.chunks)
                def _():
                    act_chunk(c + issued).start()

                act_chunk(c).wait_recv()
                rows = pl.ds(pl.multiple_of(c * CHUNK, CHUNK), CHUNK)
                added = self.arrived[rows, :].astype(F32) + self.update[rows, :]
                self.acts_v[rows, :] = added.astype(BF16)
                acts_out(c).start()

        before = self.chunks * 3 // 4
        add_chunks(0, before)
        for copy in tok_dp_copies + ug_dp_copies + dg_dp_copies:
            copy.wait_recv()
        self.tok_dp[0] = self.tok[...]
        self.place(self.dg_dp, self.gd_v, me["dp"])
        self.place(self.ug_dp, self.gu_v, me["dp"])
        stores = [
            pltpu.make_async_copy(self.gd_v, gd.at[0], self.store_sem.at[0]),
            pltpu.make_async_copy(self.gu_v, gu.at[0], self.store_sem.at[1]),
        ]
        for store in stores:
            store.start()
        add_chunks(before, self.chunks)

        for store in stores:
            store.wait()
        for copy in sent:
            copy.wait_send()

        @pl.loop(0, self.chunks)
        def _(c):
            act_chunk(c).wait_send()
            acts_out(c).wait()

    def window(self, tile):
        return max(0, tile * TILE - MAX_SEG), (tile + 1) * TILE

    def prepare_attention(self):
        blocks, pads = self.meta[:2]
        bounds = seg_bounds(blocks, pads, 0)
        for head in range(self.kv_heads):
            self.v_ones[head, :, :HD] = self.kv_v[1, :, head * HD : (head + 1) * HD]
            self.v_ones[head, :, HD:] = jnp.ones((self.length, HD), BF16)
        for tile in range(self.length // TILE):
            first, last = self.window(tile)
            here = slice(tile * TILE, (tile + 1) * TILE)
            rows = tile * TILE + lax.broadcasted_iota(jnp.int32, (TILE, last - first), 0)
            cols = first + lax.broadcasted_iota(jnp.int32, (TILE, last - first), 1)
            starts = by_segment(rows, bounds, [b[0] for b in bounds])
            ends = by_segment(rows, bounds, [b[2] for b in bounds])
            seen = (cols >= starts) & (cols <= rows) & (cols < ends)
            self.bias[here, : last - first] = jnp.where(seen, 0.0, -1e30)
            rows = tile * TILE + lax.broadcasted_iota(jnp.int32, (TILE, HD), 0)
            ends = by_segment(rows, bounds, [b[2] for b in bounds])
            self.live[here, :] = jnp.where(rows < ends, 1.0, 0.0)

    def attend(self, step):
        factor = math.log2(math.e) / math.sqrt(HD)
        span = STEP_HEADS * HD
        base = pl.multiple_of(step * span, span)
        head = step // self.steps_per_kv
        key_cols = pl.ds(pl.multiple_of(head * HD, HD), HD)
        for tile in range(self.length // TILE):
            first, last = self.window(tile)
            here = slice(tile * TILE, (tile + 1) * TILE)
            block = self.q_v[here, pl.ds(base, span)]
            for two in range(0, STEP_HEADS, 2):
                queries = jnp.concatenate(
                    [block[:, h * HD : (h + 1) * HD] for h in (two, two + 1)], axis=0
                )
                scores = dot(queries, self.kv_v[0, first:last, key_cols], (1, 1))
                scores = scores.reshape(2, TILE, last - first)
                scores = scores * factor + self.bias[here, : last - first][None]
                top = jnp.max(scores, axis=-1, keepdims=True)
                weights = jnp.exp2(scores - top).astype(BF16).reshape(2 * TILE, last - first)
                mixed = dot(weights, self.v_ones[head, first:last, :], (1, 0))
                for i, h in enumerate((two, two + 1)):
                    part = mixed[i * TILE : (i + 1) * TILE]
                    value = part[:, :HD] * (self.live[here, :] / part[:, HD:])
                    self.att[here, h * HD : (h + 1) * HD] = value.astype(BF16)
        right = self.down_v[:, :, pl.ds(base, span)].reshape(self.rows, span)
        self.acc[...] += dot(self.att[...], right, (1, 1))

    def place(self, compact, out, my_dp):
        rank, n = self.rank, self.length

        @pl.loop(0, self.width // n)
        def _(i):
            cols = pl.ds(pl.multiple_of(i * n, n), n)
            totals = [jnp.zeros((rank, n), F32)] * self.slots
            for d in range(self.dps):
                k = lax.rem(my_dp - d + self.dps, self.dps)
                for s in range(self.segs):
                    key = self.tok_dp[k, s + 1 : s + 2, :]
                    rows = compact[k, s * rank : (s + 1) * rank, cols].astype(F32)
                    for slot in range(self.slots):
                        totals[slot] = totals[slot] + jnp.where(key == slot, rows, 0.0)
            for slot in range(self.slots):
                out[slot, :, cols] = totals[slot].astype(BF16)


def per_device(sizes, act, grad, queries, keys_values, saved, down, up, blocks, pads, tenant, table):
    kernel = Kernel(sizes, (queries.shape, keys_values.shape[-1], up.shape, blocks.shape[-1]))
    scratch = kernel.scratch()
    names = list(scratch)

    def body(*refs):
        kernel(*refs[: -len(names)], **dict(zip(names, refs[-len(names) :])))

    return tuple(
        pl.pallas_call(
            body,
            out_shape=[jax.ShapeDtypeStruct(a.shape, BF16) for a in (act, down, up)],
            in_specs=[SMEM] * 4 + [pl.BlockSpec(memory_space=pl.ANY)] * 7,
            out_specs=[pl.BlockSpec(memory_space=pl.ANY)] * 3,
            scratch_shapes=list(scratch.values()),
            compiler_params=pltpu.CompilerParams(
                vmem_limit_bytes=VMEM_BYTES, collective_id=0, has_side_effects=True
            ),
            name="adapter_step",
        )(blocks, pads, tenant, table, act, grad, queries, keys_values, saved, down, up)
    )


def solution(mesh):
    wide = P("section", "dp", "tensor")
    adapter = P("section", None, None, "tensor")
    per_segment = P("section", None, "dp", None)
    return jax.shard_map(
        functools.partial(per_device, dict(mesh.shape)),
        mesh=mesh,
        in_specs=(
            wide,
            wide,
            wide,
            P("section", None, "dp", "tensor"),
            wide,
            adapter,
            adapter,
            per_segment,
            per_segment,
            per_segment,
            P(),
        ),
        out_specs=(wide, adapter, adapter),
        check_vma=False,
    )
```

time: 238 us -> 73.9 us (0.31)
  blocking collectives: 104 us -> 0 us
  Pallas kernels: 0 us -> 66.3 us
  matrix products: 57.5 us -> 0 us
  waiting for transfers between devices: 44.9 us -> 0 us
  between operations: 14.2 us -> 0.66 us
  other arithmetic: 5.24 us -> 0 us
  starting transfers between devices: 2.47 us -> 0 us
    psum x2 -> x0, blocking collectives: 104 us -> none  [the longest x1 83.8 us: per_device(): lax.psum((contract(spread_gradient, saved_rows), contract(spread_rank, ma...]
    pallas_call x0 -> x1, Pallas kernels: none -> 66.3 us  [per_device(): pl.pallas_call(body, out_shape=[jax.ShapeDtypeStruct(a.shape, BF16) for a...]
    ppermute x2 -> x0, waiting for transfers between devices: 39.2 us -> none  [from_behind(): return lax.ppermute(value, axis, pairs)]
    dot_general x7 -> x0, matrix products: 35.2 us -> none  [the longest x1 14 us: one_block(): jnp.einsum('hgqk,khd->qhgd', weights, value_heads, preferred_element_type...]
    sub x1 -> x0, matrix products: 22.3 us -> none  [one_block(): exponent = jnp.where(allowed, jnp.exp(masked_scores - row_top), 0.0)]
    psum x1 -> x0, waiting for transfers between devices: 5.71 us -> none  [per_device(): lax.psum((contract(spread_gradient, saved_rows), contract(spread_rank, ma...]
    convert_element_type x9 -> x0, other arithmetic: 2.78 us -> none  [the longest x1 2.7 us: per_device(): (adapter_scale * up_gradient).reshape(output_layout).astype(jnp.bfloat16)]
    ppermute x2 -> x0, starting transfers between devices: 2.43 us -> none  [from_behind(): return lax.ppermute(value, axis, pairs)]
  transfers between devices with their start and end apart: 3 -> 0, of which waited for: 2 -> 0; matrix products, arithmetic and copies ran while one was open for 29% -> 0% of each run, Pallas kernels for 0% -> 0%
where the time goes in v2:
time: 73.9 us; the launch traced here: 73.7 us
  Pallas kernels  66.3 us (90%)
  local copies, waits for them, and re-layouts  6.79 us (9%)
    pallas_call x1, Pallas kernels, per_device(): pl.pallas_call(body, out_shape=[jax.ShapeDtypeStruct(a.shape, BF16) for a...  66.3 us
    unnamed x7, local copies, waits for them, and re-layouts  6.79 us

profile of v2, /device:TPU:0, one launch (start us, length us, event | category | flops | bytes accessed | tf_op | source)
XLA Modules:
  0.0 73.7 jit_solution(4489931491889053667)
XLA Ops:
  0.6 66.3 %adapter_step.1 = (bf16[1,512,4096]{2,1,0:T(8,128)(2,1)}, bf16[1,8,16,4096]{3,2,1,0:T(8,128)(2,1)}, bf16[1,8,16,4096]{3,2,1,0:T(8,128)(2,1)}) custom-call(s32[1,2,1,3]{3,2,1,0:T(1,128)} %refs_0_.1, s32[1,2,1,3]{3,2,1,0:T(1,128)} %refs_1_.1, s32[1,2,1,3]{3,2,1,0:T(1,128)} %refs_2_.1, s32[32]{0:T(128)} %refs_3_.1, bf16[1,512,4096]{2,1,0:T(8,128)(2,1)} %refs_4_.1, ...), custom_call_target="tpu_custom_call" | custom-call | tf_op jit(solution)/shard_map/adapter_step/pallas_call | solution.py:429
  66.9 0.0 copy-start.1
  66.9 0.0 copy-start
  66.9 4.8 %copy.17 = bf16[1,512,4096]{2,1,0:T(8,128)(2,1)} copy(bf16[1,512,4096]{2,1,0:T(8,128)(2,1)} %get-tuple-element.6) | data formatting | bytes 8388608
  71.8 0.0 copy-done.1
  71.8 1.0 %copy.18 = bf16[1,8,16,4096]{3,2,1,0:T(8,128)(2,1)} copy(bf16[1,8,16,4096]{3,2,1,0:T(8,128)(2,1)S(1)} %copy-done.1) | data formatting | bytes 2097152
  72.8 0.0 copy-done
  72.8 1.0 %copy.19 = bf16[1,8,16,4096]{3,2,1,0:T(8,128)(2,1)} copy(bf16[1,8,16,4096]{3,2,1,0:T(8,128)(2,1)S(1)} %copy-done) | data formatting | bytes 2097152
Async XLA Ops:
  66.9 4.9 %copy-start.1 = (bf16[1,8,16,4096]{3,2,1,0:T(8,128)(2,1)S(1)}, bf16[1,8,16,4096]{3,2,1,0:T(8,128)(2,1)}, u32[]{:S(2)}) copy-start(bf16[1,8,16,4096]{3,2,1,0:T(8,128)(2,1)} %get-tuple-element.7) | copy-start | bytes 3145732
  66.9 5.8 %copy-start = (bf16[1,8,16,4096]{3,2,1,0:T(8,128)(2,1)S(1)}, bf16[1,8,16,4096]{3,2,1,0:T(8,128)(2,1)}, u32[]{:S(2)}) copy-start(bf16[1,8,16,4096]{3,2,1,0:T(8,128)(2,1)} %get-tuple-element.8) | copy-start | bytes 3145732

commit v3 on v2

--- a/solution.py
+++ b/solution.py
@@ -15,7 +15,7 @@
 SCALE = 2.0
 F32 = jnp.float32
 BF16 = jnp.bfloat16
-VMEM_BYTES = 60 * 1024 * 1024
+VMEM_BYTES = 50 * 1024 * 1024
 CHUNK = 32
 COLS = 1024
 STEP_HEADS = 4
@@ -80,6 +80,7 @@
         adapter = pltpu.VMEM((self.slots, r, w), BF16)
         ranks = pltpu.VMEM((self.tensors, r, n), F32)
         one = pltpu.VMEM((r, n), F32)
+        half = pltpu.VMEM((r, n), BF16)
         return dict(
             up_v=adapter,
             down_v=adapter,
@@ -94,8 +95,12 @@
             tok_dp=pltpu.VMEM((self.dps, 8, n), jnp.int32),
             back_send=one,
             back_in=ranks,
+            back_sum=half,
+            back_there=half,
             gp_send=one,
             gp_in=ranks,
+            gp_sum=half,
+            gp_there=half,
             fwd_send=one,
             fwd_in=ranks,
             ug_send=pltpu.VMEM((p, w), BF16),
@@ -103,23 +108,20 @@
             dg_dp=pltpu.VMEM((self.dps, p, w), BF16),
             arrived=wide,
             update=pltpu.VMEM((n, w), F32),
-            acts_v=wide,
-            gd_v=adapter,
-            gu_v=adapter,
             acc=pltpu.VMEM((n, self.rows), F32),
             bias=pltpu.VMEM((n, MAX_SEG + TILE), F32),
             live=pltpu.VMEM((n, HD), F32),
             v_ones=pltpu.VMEM((self.kv_heads, n, 2 * HD), BF16),
             att=pltpu.VMEM((n, STEP_HEADS * HD), BF16),
             load_sem=dma((6,)),
-            store_sem=dma((2,)),
-            acts_sem=dma((self.chunks,)),
             up_sem=dma((2,)),
             tok_sem=dma((2,)),
             tok_dp_sem=dma((2, self.dps)),
             back_sem=dma((2, self.tensors)),
             gp_sem=dma((2, self.tensors)),
             fwd_sem=dma((2, self.tensors)),
+            back_sum_sem=dma((2,)),
+            gp_sum_sem=dma((2,)),
             ug_sem=dma((2,)),
             ug_dp_sem=dma((2, self.dps)),
             dg_dp_sem=dma((2, self.dps)),
@@ -175,7 +177,7 @@
             load.start()
 
         barrier = pltpu.get_barrier_semaphore()
-        partners = [device(section=s, tensor=k) for s in (1, -1) for k in range(self.tensors)]
+        partners = [device(section=s) for s in (1, -1)]
         partners += [device(tensor=k) for k in range(1, self.tensors)]
         partners += [device(dp=k) for k in range(1, self.dps)]
         for partner in partners:
@@ -206,6 +208,18 @@
             sent.append(copy)
             return copy
 
+        def to_tensor(part, source, target, sem):
+            source[...] = part
+            return [
+                start(send(source, target.at[k], pair(sem, k), device(tensor=k)))
+                for k in range(1, self.tensors)
+            ]
+
+        def tensor_sum(copies, source, target):
+            for copy in copies:
+                copy.wait_recv()
+            return source[...] + sum(target[k] for k in range(1, self.tensors))
+
         up_copy = start(send(self.up_send, self.up_in, (self.up_sem.at[0], self.up_sem.at[1]), device(section=1)))
         tok_copy = start(send(self.tok, self.tok_in, (self.tok_sem.at[0], self.tok_sem.at[1]), device(section=1)))
         act_chunk(0).start()
@@ -224,17 +238,15 @@
             right = self.down_v[:, :, cols].reshape(self.rows, COLS)
             self.acc[...] += dot(self.saved_v[:, cols], right, (1, 1))
 
-        self.back_send[...] = select_rows(self.acc[...].T, range(self.slots), back_slot, rank)
-        back_copies = [
-            start(send(self.back_send, self.back_in.at[k], pair(self.back_sem, k), device(section=1, tensor=k)))
-            for k in range(self.tensors)
-        ]
+        back_part = select_rows(self.acc[...].T, range(self.slots), back_slot, rank)
+        back_copies = to_tensor(back_part, self.back_send, self.back_in, self.back_sem)
         act_chunk(1).start()
 
         loads[3].wait()
         loads[4].wait()
         self.prepare_attention()
         self.acc[...] = jnp.zeros_like(self.acc)
+        few = max(1, self.steps // 8)
         early, late = self.steps * 3 // 8, self.steps * 7 // 8
 
         def attend_steps(first, last):
@@ -243,15 +255,19 @@
                 self.attend(step)
                 act_chunk(2 + step).start()
 
-        attend_steps(0, early)
+        attend_steps(0, few)
+        self.back_sum[...] = tensor_sum(back_copies, self.back_send, self.back_in).astype(BF16)
+        back_copy = start(
+            send(self.back_sum, self.back_there, (self.back_sum_sem.at[0], self.back_sum_sem.at[1]), device(section=1))
+        )
+        attend_steps(few, early)
 
         loads[5].wait()
         up_copy.wait_recv()
         tok_copy.wait_recv()
-        for copy in back_copies:
-            copy.wait_recv()
+        back_copy.wait_recv()
         seg_row = self.tok_in[0:1, :]
-        total = sum(self.back_in[k] for k in range(self.tensors)).astype(BF16).astype(F32)
+        total = self.back_there[...].astype(F32)
         spread = spread_rows(total, range(self.segs), seg_row).astype(BF16)
         fill = jnp.zeros((self.rows - self.packed, COLS), BF16)
         full = jnp.zeros((n, self.rows), F32)
@@ -260,24 +276,26 @@
             block = self.grad_v[:, cols]
             full = full + dot(block, jnp.concatenate([self.up_in[:, cols], fill], axis=0), (1, 1))
             self.ug_send[:, cols] = (SCALE * dot(spread, block, (1, 0))).astype(BF16)
-        self.gp_send[...] = select_rows(full.T, range(self.segs), seg_row, rank)
-        gp_copies = [
-            start(send(self.gp_send, self.gp_in.at[k], pair(self.gp_sem, k), device(section=-1, tensor=k)))
-            for k in range(self.tensors)
-        ]
+        gp_part = select_rows(full.T, range(self.segs), seg_row, rank)
+        gp_copies = to_tensor(gp_part, self.gp_send, self.gp_in, self.gp_sem)
         ug_copy = start(send(self.ug_send, self.ug_dp.at[0], (self.ug_sem.at[0], self.ug_sem.at[1]), device(section=-1)))
 
-        attend_steps(early, late)
+        attend_steps(early, early + few)
+        total = tensor_sum(gp_copies, self.gp_send, self.gp_in)
+        self.gp_sum[...] = (SCALE * total).astype(BF16)
+        gp_copy = start(
+            send(self.gp_sum, self.gp_there, (self.gp_sum_sem.at[0], self.gp_sum_sem.at[1]), device(section=-1))
+        )
+        attend_steps(early + few, late)
 
         ug_copy.wait_recv()
         ug_dp_copies = [
             start(send(self.ug_dp.at[0], self.ug_dp.at[k], pair(self.ug_dp_sem, k), device(dp=k)))
             for k in range(1, self.dps)
         ]
-        for copy in gp_copies:
-            copy.wait_recv()
-        total = SCALE * sum(self.gp_in[k] for k in range(self.tensors))
-        spread = spread_rows(total.astype(BF16).astype(F32), range(self.segs), self.tok[0:1, :]).astype(BF16)
+        gp_copy.wait_recv()
+        total = self.gp_there[...].astype(F32)
+        spread = spread_rows(total, range(self.segs), self.tok[0:1, :]).astype(BF16)
         for i in range(w // COLS):
             cols = slice(i * COLS, (i + 1) * COLS)
             self.dg_dp[0, :, cols] = dot(spread, self.saved_v[:, cols], (1, 0)).astype(BF16)
@@ -291,15 +309,8 @@
         bounds = seg_bounds(blocks, pads, 0)
         fwd_slot = by_segment(tokens, bounds, seg_slots(tenant, table, 0))
         fwd_part = select_rows(self.acc[...].T, range(self.slots), fwd_slot, rank)
-        self.fwd_send[...] = fwd_part
-        fwd_copies = [
-            start(send(self.fwd_send, self.fwd_in.at[k], pair(self.fwd_sem, k), device(tensor=k)))
-            for k in range(1, self.tensors)
-        ]
-        for copy in fwd_copies:
-            copy.wait_recv()
-        total = fwd_part + sum(self.fwd_in[k] for k in range(1, self.tensors))
-        total = total.astype(BF16).astype(F32)
+        fwd_copies = to_tensor(fwd_part, self.fwd_send, self.fwd_in, self.fwd_sem)
+        total = tensor_sum(fwd_copies, self.fwd_send, self.fwd_in).astype(BF16).astype(F32)
         spread = spread_rows(total, range(self.slots), fwd_slot).T.astype(BF16)
         for i in range(w // COLS):
             cols = slice(i * COLS, (i + 1) * COLS)
@@ -307,10 +318,6 @@
             self.update[:, cols] = SCALE * dot(spread, right, (1, 0))
 
         issued = 2 + self.steps
-
-        def acts_out(c):
-            rows = pl.ds(pl.multiple_of(c * CHUNK, CHUNK), CHUNK)
-            return pltpu.make_async_copy(self.acts_v.at[rows, :], acts.at[0, rows, :], self.acts_sem.at[c])
 
         def add_chunks(first, last):
             @pl.loop(first, last)
@@ -322,33 +329,23 @@
                 act_chunk(c).wait_recv()
                 rows = pl.ds(pl.multiple_of(c * CHUNK, CHUNK), CHUNK)
                 added = self.arrived[rows, :].astype(F32) + self.update[rows, :]
-                self.acts_v[rows, :] = added.astype(BF16)
-                acts_out(c).start()
+                acts[0, rows, :] = added.astype(BF16)
 
         before = self.chunks * 3 // 4
         add_chunks(0, before)
         for copy in tok_dp_copies + ug_dp_copies + dg_dp_copies:
             copy.wait_recv()
         self.tok_dp[0] = self.tok[...]
-        self.place(self.dg_dp, self.gd_v, me["dp"])
-        self.place(self.ug_dp, self.gu_v, me["dp"])
-        stores = [
-            pltpu.make_async_copy(self.gd_v, gd.at[0], self.store_sem.at[0]),
-            pltpu.make_async_copy(self.gu_v, gu.at[0], self.store_sem.at[1]),
-        ]
-        for store in stores:
-            store.start()
+        self.place(self.dg_dp, gd, me["dp"])
+        self.place(self.ug_dp, gu, me["dp"])
         add_chunks(before, self.chunks)
 
-        for store in stores:
-            store.wait()
         for copy in sent:
             copy.wait_send()
 
         @pl.loop(0, self.chunks)
         def _(c):
             act_chunk(c).wait_send()
-            acts_out(c).wait()
 
     def window(self, tile):
         return max(0, tile * TILE - MAX_SEG), (tile + 1) * TILE
@@ -414,7 +411,7 @@
                     for slot in range(self.slots):
                         totals[slot] = totals[slot] + jnp.where(key == slot, rows, 0.0)
             for slot in range(self.slots):
-                out[slot, :, cols] = totals[slot].astype(BF16)
+                out[0, slot, :, cols] = totals[slot].astype(BF16)
 
 
 def per_device(sizes, act, grad, queries, keys_values, saved, down, up, blocks, pads, tenant, table):
@@ -428,15 +425,24 @@
     return tuple(
         pl.pallas_call(
             body,
-            out_shape=[jax.ShapeDtypeStruct(a.shape, BF16) for a in (act, down, up)],
+            out_shape=[pltpu.VMEM(a.shape, BF16) for a in (act, down, up)],
             in_specs=[SMEM] * 4 + [pl.BlockSpec(memory_space=pl.ANY)] * 7,
-            out_specs=[pl.BlockSpec(memory_space=pl.ANY)] * 3,
+            out_specs=[pl.BlockSpec(memory_space=pltpu.VMEM)] * 3,
             scratch_shapes=list(scratch.values()),
             compiler_params=pltpu.CompilerParams(
                 vmem_limit_bytes=VMEM_BYTES, collective_id=0, has_side_effects=True
             ),
             name="adapter_step",
-        )(blocks, pads, tenant, table, act, grad, queries, keys_values, saved, down, up)
+        )(
+            blocks,
+            pads,
+            tenant,
+            table,
+            *[
+                pltpu.with_memory_space_constraint(a, pltpu.HBM)
+                for a in (act, grad, queries, keys_values, saved, down, up)
+            ],
+        )
     )
 
 

time: 73.9 us -> 67.3 us (0.911)
  Pallas kernels: 66.3 us -> 62.5 us
  local copies, waits for them, and re-layouts: 6.79 us -> 3.95 us
    pallas_call x1, Pallas kernels: 66.3 us -> 62.5 us  [per_device(): pl.pallas_call(body, out_shape=[pltpu.VMEM(a.shape, BF16) for a in (act,...]
    unnamed x7 -> x3, local copies, waits for them, and re-layouts: 6.79 us -> 3.95 us
where the time goes in v3:
time: 67.3 us; the launch traced here: 67.1 us
  Pallas kernels  62.5 us (93%)
  local copies, waits for them, and re-layouts  3.95 us (6%)
    pallas_call x1, Pallas kernels, per_device(): pl.pallas_call(body, out_shape=[pltpu.VMEM(a.shape, BF16) for a in (act,...  62.5 us
    unnamed x3, local copies, waits for them, and re-layouts  3.95 us

profile of v3, /device:TPU:0, one launch (start us, length us, event | category | flops | bytes accessed | tf_op | source)
XLA Modules:
  0.0 67.1 jit_solution(14429229484386674351)
XLA Ops:
  0.6 62.5 %adapter_step.1 = (bf16[1,512,4096]{2,1,0:T(8,128)(2,1)S(1)}, bf16[1,8,16,4096]{3,2,1,0:T(8,128)(2,1)S(1)}, bf16[1,8,16,4096]{3,2,1,0:T(8,128)(2,1)S(1)}) custom-call(s32[1,2,1,3]{3,2,1,0:T(1,128)} %refs_0_.1, s32[1,2,1,3]{3,2,1,0:T(1,128)} %refs_1_.1, s32[1,2,1,3]{3,2,1,0:T(1,128)} %refs_2_.1, s32[32]{0:T(128)} %refs_3_.1, bf16[1,512,4096]{2,1,0:T(8,128)(2,1)} %refs_4_.1, ...), custom_call_target="tpu_custom_call" | custom-call | tf_op jit(solution)/shard_map/adapter_step/pallas_call | solution.py:426
  63.2 2.0 %copy.17 = bf16[1,512,4096]{2,1,0:T(8,128)(2,1)} copy(bf16[1,512,4096]{2,1,0:T(8,128)(2,1)S(1)} %get-tuple-element.3) | data formatting | bytes 8388608
  65.2 1.0 %copy.18 = bf16[1,8,16,4096]{3,2,1,0:T(8,128)(2,1)} copy(bf16[1,8,16,4096]{3,2,1,0:T(8,128)(2,1)S(1)} %get-tuple-element.4) | data formatting | bytes 2097152
  66.2 1.0 %copy.19 = bf16[1,8,16,4096]{3,2,1,0:T(8,128)(2,1)} copy(bf16[1,8,16,4096]{3,2,1,0:T(8,128)(2,1)S(1)} %get-tuple-element.5) | data formatting | bytes 2097152

commit v4 on v3

--- a/solution.py
+++ b/solution.py
@@ -19,6 +19,7 @@
 CHUNK = 32
 COLS = 1024
 STEP_HEADS = 4
+WRITES = 4
 
 SMEM = pl.BlockSpec(memory_space=pltpu.SMEM)
 
@@ -108,12 +109,17 @@
             dg_dp=pltpu.VMEM((self.dps, p, w), BF16),
             arrived=wide,
             update=pltpu.VMEM((n, w), F32),
+            acts_v=wide,
+            gd_v=adapter,
+            gu_v=adapter,
             acc=pltpu.VMEM((n, self.rows), F32),
             bias=pltpu.VMEM((n, MAX_SEG + TILE), F32),
             live=pltpu.VMEM((n, HD), F32),
             v_ones=pltpu.VMEM((self.kv_heads, n, 2 * HD), BF16),
             att=pltpu.VMEM((n, STEP_HEADS * HD), BF16),
             load_sem=dma((6,)),
+            store_sem=dma((2,)),
+            acts_sem=dma((self.chunks,)),
             up_sem=dma((2,)),
             tok_sem=dma((2,)),
             tok_dp_sem=dma((2, self.dps)),
@@ -158,6 +164,15 @@
             rows = pl.ds(pl.multiple_of(c * CHUNK, CHUNK), CHUNK)
             return send(
                 act.at[0, rows, :], self.arrived.at[rows, :], pair(self.act_sem, c), device(section=1)
+            )
+
+        barrier = pltpu.get_barrier_semaphore()
+        partners = [device(section=s) for s in (1, -1)]
+        partners += [device(tensor=k) for k in range(1, self.tensors)]
+        partners += [device(dp=k) for k in range(1, self.dps)]
+        for partner in partners:
+            pl.semaphore_signal(
+                barrier, inc=1, device_id=partner, device_id_type=pl.DeviceIdType.MESH
             )
 
         loads = [
@@ -176,15 +191,6 @@
         for load in loads:
             load.start()
 
-        barrier = pltpu.get_barrier_semaphore()
-        partners = [device(section=s) for s in (1, -1)]
-        partners += [device(tensor=k) for k in range(1, self.tensors)]
-        partners += [device(dp=k) for k in range(1, self.dps)]
-        for partner in partners:
-            pl.semaphore_signal(
-                barrier, inc=1, device_id=partner, device_id_type=pl.DeviceIdType.MESH
-            )
-
         tokens = token_row(n)
         bounds = seg_bounds(blocks, pads, 1)
         slots = seg_slots(tenant, table, 1)
@@ -200,6 +206,7 @@
         for i, slot in enumerate(slots):
             self.up_send[i * rank : (i + 1) * rank, :] = self.up_v[slot]
         pl.semaphore_wait(barrier, len(partners))
+        act_chunk(0).start()
 
         sent = []
 
@@ -222,7 +229,6 @@
 
         up_copy = start(send(self.up_send, self.up_in, (self.up_sem.at[0], self.up_sem.at[1]), device(section=1)))
         tok_copy = start(send(self.tok, self.tok_in, (self.tok_sem.at[0], self.tok_sem.at[1]), device(section=1)))
-        act_chunk(0).start()
         tok_dp_copies = [
             start(send(self.tok, self.tok_dp.at[k], pair(self.tok_dp_sem, k), device(dp=k)))
             for k in range(1, self.dps)
@@ -319,6 +325,10 @@
 
         issued = 2 + self.steps
 
+        def acts_out(c):
+            rows = pl.ds(pl.multiple_of(c * CHUNK, CHUNK), CHUNK)
+            return pltpu.make_async_copy(self.acts_v.at[rows, :], acts.at[0, rows, :], self.acts_sem.at[c])
+
         def add_chunks(first, last):
             @pl.loop(first, last)
             def _(c):
@@ -329,23 +339,33 @@
                 act_chunk(c).wait_recv()
                 rows = pl.ds(pl.multiple_of(c * CHUNK, CHUNK), CHUNK)
                 added = self.arrived[rows, :].astype(F32) + self.update[rows, :]
-                acts[0, rows, :] = added.astype(BF16)
+                self.acts_v[rows, :] = added.astype(BF16)
+                acts_out(c).start()
 
         before = self.chunks * 3 // 4
         add_chunks(0, before)
         for copy in tok_dp_copies + ug_dp_copies + dg_dp_copies:
             copy.wait_recv()
         self.tok_dp[0] = self.tok[...]
-        self.place(self.dg_dp, gd, me["dp"])
-        self.place(self.ug_dp, gu, me["dp"])
+        self.place(self.dg_dp, self.gd_v, me["dp"])
+        self.place(self.ug_dp, self.gu_v, me["dp"])
+        stores = [
+            pltpu.make_async_copy(self.gd_v, gd.at[0], self.store_sem.at[0]),
+            pltpu.make_async_copy(self.gu_v, gu.at[0], self.store_sem.at[1]),
+        ]
+        for store in stores:
+            store.start()
         add_chunks(before, self.chunks)
 
+        for store in stores:
+            store.wait()
         for copy in sent:
             copy.wait_send()
 
         @pl.loop(0, self.chunks)
         def _(c):
             act_chunk(c).wait_send()
+            acts_out(c).wait()
 
     def window(self, tile):
         return max(0, tile * TILE - MAX_SEG), (tile + 1) * TILE
@@ -411,7 +431,7 @@
                     for slot in range(self.slots):
                         totals[slot] = totals[slot] + jnp.where(key == slot, rows, 0.0)
             for slot in range(self.slots):
-                out[0, slot, :, cols] = totals[slot].astype(BF16)
+                out[slot, :, cols] = totals[slot].astype(BF16)
 
 
 def per_device(sizes, act, grad, queries, keys_values, saved, down, up, blocks, pads, tenant, table):
@@ -422,12 +442,12 @@
     def body(*refs):
         kernel(*refs[: -len(names)], **dict(zip(names, refs[-len(names) :])))
 
-    return tuple(
+    held = (
         pl.pallas_call(
             body,
             out_shape=[pltpu.VMEM(a.shape, BF16) for a in (act, down, up)],
             in_specs=[SMEM] * 4 + [pl.BlockSpec(memory_space=pl.ANY)] * 7,
-            out_specs=[pl.BlockSpec(memory_space=pltpu.VMEM)] * 3,
+            out_specs=[pl.BlockSpec(memory_space=pl.ANY)] * 3,
             scratch_shapes=list(scratch.values()),
             compiler_params=pltpu.CompilerParams(
                 vmem_limit_bytes=VMEM_BYTES, collective_id=0, has_side_effects=True
@@ -444,6 +464,33 @@
             ],
         )
     )
+    return tuple(
+        pl.pallas_call(
+            write_kernel,
+            out_shape=[jax.ShapeDtypeStruct(a.shape, BF16) for a in held],
+            in_specs=[pl.BlockSpec(memory_space=pl.ANY)] * 3,
+            out_specs=[pl.BlockSpec(memory_space=pl.ANY)] * 3,
+            scratch_shapes=[pltpu.SemaphoreType.DMA((WRITES + 2,))],
+            compiler_params=pltpu.CompilerParams(vmem_limit_bytes=2 * 1024 * 1024),
+            name="write_results",
+        )(*[pltpu.with_memory_space_constraint(a, pltpu.VMEM) for a in held])
+    )
+
+
+def write_kernel(acts_v, gd_v, gu_v, acts, gd, gu, sem):
+    rows = acts.shape[1] // WRITES
+    copies = [
+        pltpu.make_async_copy(
+            acts_v.at[0, i * rows : (i + 1) * rows], acts.at[0, i * rows : (i + 1) * rows], sem.at[i]
+        )
+        for i in range(WRITES)
+    ]
+    copies.append(pltpu.make_async_copy(gd_v, gd, sem.at[WRITES]))
+    copies.append(pltpu.make_async_copy(gu_v, gu, sem.at[WRITES + 1]))
+    for copy in copies:
+        copy.start()
+    for copy in copies:
+        copy.wait()
 
 
 def solution(mesh):

time: 67.3 us -> 66.5 us (0.988)
  local copies, waits for them, and re-layouts: 3.95 us -> 0 us
  Pallas kernels: 62.5 us -> 65.7 us
    unnamed x3 -> x0, local copies, waits for them, and re-layouts: 3.95 us -> none
    pallas_call x0 -> x1, Pallas kernels: none -> 2.72 us  [per_device(): pl.pallas_call(write_kernel, out_shape=[jax.ShapeDtypeStruct(a.shape, BF1...]
where the time goes in v4:
time: 66.5 us; the launch traced here: 66.3 us
  Pallas kernels  65.7 us (99%)
    pallas_call x1, Pallas kernels, per_device(): pl.pallas_call(body, out_shape=[pltpu.VMEM(a.shape, BF16) for a in (act,...  62.9 us
    pallas_call x1, Pallas kernels, per_device(): pl.pallas_call(write_kernel, out_shape=[jax.ShapeDtypeStruct(a.shape, BF1...  2.72 us

profile of v4, /device:TPU:0, one launch (start us, length us, event | category | flops | bytes accessed | tf_op | source)
XLA Modules:
  0.0 66.3 jit_solution(5873401059571979013)
XLA Ops:
  0.6 62.9 %adapter_step.1 = (bf16[1,512,4096]{2,1,0:T(8,128)(2,1)S(1)}, bf16[1,8,16,4096]{3,2,1,0:T(8,128)(2,1)S(1)}, bf16[1,8,16,4096]{3,2,1,0:T(8,128)(2,1)S(1)}) custom-call(s32[1,2,1,3]{3,2,1,0:T(1,128)} %refs_0_.1, s32[1,2,1,3]{3,2,1,0:T(1,128)} %refs_1_.1, s32[1,2,1,3]{3,2,1,0:T(1,128)} %refs_2_.1, s32[32]{0:T(128)} %refs_3_.1, bf16[1,512,4096]{2,1,0:T(8,128)(2,1)} %refs_4_.1, ...), custom_call_target="tpu_custom_call" | custom-call | tf_op jit(solution)/shard_map/adapter_step/pallas_call | solution.py:446
  63.6 2.7 %write_results.1 = (bf16[1,512,4096]{2,1,0:T(8,128)(2,1)}, bf16[1,8,16,4096]{3,2,1,0:T(8,128)(2,1)}, bf16[1,8,16,4096]{3,2,1,0:T(8,128)(2,1)}) custom-call(bf16[1,512,4096]{2,1,0:T(8,128)(2,1)S(1)} %get-tuple-element.6.acts_v, bf16[1,8,16,4096]{3,2,1,0:T(8,128)(2,1)S(1)} %get-tuple-element.7.gd_v, bf16[1,8,16,4096]{3,2,1,0:T(8,128)(2,1)S(1)} %get-tuple-element.8.gu_v), custom_call_target="tpu_custom_call" | custom-call | tf_op jit(solution)/shard_map/write_results/pallas_call | solution.py:468

commit v5 on v4

--- a/solution.py
+++ b/solution.py
@@ -255,18 +255,20 @@
         few = max(1, self.steps // 8)
         early, late = self.steps * 3 // 8, self.steps * 7 // 8
 
-        def attend_steps(first, last):
+        def attend_steps(first, last, ahead):
             @pl.loop(first, last)
             def _(step):
                 self.attend(step)
-                act_chunk(2 + step).start()
-
-        attend_steps(0, few)
+                act_chunk(ahead + step).start()
+
+        attend_steps(0, few, 2)
         self.back_sum[...] = tensor_sum(back_copies, self.back_send, self.back_in).astype(BF16)
         back_copy = start(
             send(self.back_sum, self.back_there, (self.back_sum_sem.at[0], self.back_sum_sem.at[1]), device(section=1))
         )
-        attend_steps(few, early)
+        act_chunk(few + 2).start()
+        attend_steps(few, early, 3)
+        act_chunk(early + 3).start()
 
         loads[5].wait()
         up_copy.wait_recv()
@@ -286,13 +288,13 @@
         gp_copies = to_tensor(gp_part, self.gp_send, self.gp_in, self.gp_sem)
         ug_copy = start(send(self.ug_send, self.ug_dp.at[0], (self.ug_sem.at[0], self.ug_sem.at[1]), device(section=-1)))
 
-        attend_steps(early, early + few)
+        attend_steps(early, early + few, 4)
         total = tensor_sum(gp_copies, self.gp_send, self.gp_in)
         self.gp_sum[...] = (SCALE * total).astype(BF16)
         gp_copy = start(
             send(self.gp_sum, self.gp_there, (self.gp_sum_sem.at[0], self.gp_sum_sem.at[1]), device(section=-1))
         )
-        attend_steps(early + few, late)
+        attend_steps(early + few, late, 4)
 
         ug_copy.wait_recv()
         ug_dp_copies = [
@@ -310,7 +312,7 @@
             for k in range(1, self.dps)
         ]
 
-        attend_steps(late, self.steps)
+        attend_steps(late, self.steps, 4)
 
         bounds = seg_bounds(blocks, pads, 0)
         fwd_slot = by_segment(tokens, bounds, seg_slots(tenant, table, 0))
@@ -323,7 +325,7 @@
             right = self.up_v[:, :, cols].reshape(self.rows, COLS)
             self.update[:, cols] = SCALE * dot(spread, right, (1, 0))
 
-        issued = 2 + self.steps
+        issued = 4 + self.steps
 
         def acts_out(c):
             rows = pl.ds(pl.multiple_of(c * CHUNK, CHUNK), CHUNK)

time: 66.5 us -> 66.5 us (level)
  no operation moved by 1% of the time
where the time goes in v5:
time: 66.5 us; the launch traced here: 66.3 us
  Pallas kernels  65.7 us (99%)
    pallas_call x1, Pallas kernels, per_device(): pl.pallas_call(body, out_shape=[pltpu.VMEM(a.shape, BF16) for a in (act,...  62.9 us
    pallas_call x1, Pallas kernels, per_device(): pl.pallas_call(write_kernel, out_shape=[jax.ShapeDtypeStruct(a.shape, BF1...  2.72 us

profile of v5, /device:TPU:0, one launch (start us, length us, event | category | flops | bytes accessed | tf_op | source)
XLA Modules:
  0.0 66.3 jit_solution(14120361144993403992)
XLA Ops:
  0.6 62.9 %adapter_step.1 = (bf16[1,512,4096]{2,1,0:T(8,128)(2,1)S(1)}, bf16[1,8,16,4096]{3,2,1,0:T(8,128)(2,1)S(1)}, bf16[1,8,16,4096]{3,2,1,0:T(8,128)(2,1)S(1)}) custom-call(s32[1,2,1,3]{3,2,1,0:T(1,128)} %refs_0_.1, s32[1,2,1,3]{3,2,1,0:T(1,128)} %refs_1_.1, s32[1,2,1,3]{3,2,1,0:T(1,128)} %refs_2_.1, s32[32]{0:T(128)} %refs_3_.1, bf16[1,512,4096]{2,1,0:T(8,128)(2,1)} %refs_4_.1, ...), custom_call_target="tpu_custom_call" | custom-call | tf_op jit(solution)/shard_map/adapter_step/pallas_call | solution.py:448
  63.6 2.7 %write_results.1 = (bf16[1,512,4096]{2,1,0:T(8,128)(2,1)}, bf16[1,8,16,4096]{3,2,1,0:T(8,128)(2,1)}, bf16[1,8,16,4096]{3,2,1,0:T(8,128)(2,1)}) custom-call(bf16[1,512,4096]{2,1,0:T(8,128)(2,1)S(1)} %get-tuple-element.6.acts_v, bf16[1,8,16,4096]{3,2,1,0:T(8,128)(2,1)S(1)} %get-tuple-element.7.gd_v, bf16[1,8,16,4096]{3,2,1,0:T(8,128)(2,1)S(1)} %get-tuple-element.8.gu_v), custom_call_target="tpu_custom_call" | custom-call | tf_op jit(solution)/shard_map/write_results/pallas_call | solution.py:470
